TPU v7x, 128 devices: a whole 4x4x4 slice. The times are simulated.
128 devices in a mesh: section: 4 (over x_hi, core), dom: 32 (over z, y, x_lo).
Axes of the slice: x: 4 (x_hi: 2, x_lo: 2; x = x_hi * 2 + x_lo), y: 4, z: 4, core: 2. Of those that a mesh axis runs over, the one named last changes fastest.
Arguments:
- voltages: bfloat16 [512, 64, 2048], P('dom'), may hold values from -6 to 6
- station_map: int32 [512], replicated, may hold values from 0 to 511, each once
- beam_table: int32 [128, 512], replicated, may hold values from 0 to 63
- weight_table: bfloat16 [2, 64, 1024], P(None, None, 'dom'), may hold values from -0.3125 to 0.3125
- dm_trial: int32 [128], replicated, may hold values from 0 to 31
Outputs:
- power: float32 [128, 64, 1024], P(('section', 'dom'))
Inputs may be any that keep to these rules, and one draw needn't show every extreme that they name: `station_map`: each of the 512 stations appears once.
All inputs are finite; a program needn't handle non-finite values.
Results may differ from a plain program's by a relative error of at most 0.0042.
Values may be sent and summed in bfloat16 or wider, within the bound.
No kernel may reach another device: no remote copies, remote signals or barrier semaphores. Data moves between devices by JAX's collectives and lax.ppermute only.
A program may use at most 128 MiB of HBM per device.

v0:
```python
import math

import jax
import jax.numpy as jnp
from jax import lax
from jax.sharding import PartitionSpec as P

NSTAT = 512
NFFT = 2048
CH = 1024
BEAMS = 128
NTAB = 64
FRAMES = 64
NDM = 32


def dft_table():
    sample_index = jnp.arange(NFFT, dtype=jnp.int32)
    window = 0.5 - 0.5 * jnp.cos(sample_index.astype(jnp.float32) * (2.0 * math.pi / NFFT))
    column = jnp.arange(NFFT, dtype=jnp.int32)
    bin_index = column % CH
    product = sample_index[:, None] * bin_index[None, :] % NFFT
    angle = product.astype(jnp.float32) * (2.0 * math.pi / NFFT)
    values = jnp.where(column[None, :] < CH, jnp.cos(angle), -jnp.sin(angle))
    return (values * (window[:, None] / math.sqrt(NFFT))).astype(jnp.bfloat16)


def frame_tables():
    index = jnp.arange(FRAMES, dtype=jnp.int32)
    angle = (index[:, None] * index[None, :] % FRAMES).astype(jnp.float32) * (
        2.0 * math.pi / FRAMES
    )
    cosine = jnp.cos(angle)
    sine = jnp.sin(angle)
    forward = jnp.concatenate(
        (jnp.concatenate((cosine, -sine), axis=1), jnp.concatenate((sine, cosine), axis=1)), axis=0
    )
    inverse = (
        jnp.concatenate(
            (jnp.concatenate((cosine, sine), axis=1), jnp.concatenate((-sine, cosine), axis=1)),
            axis=0,
        )
        / FRAMES
    )
    return (forward, inverse)


def dedisperse(series, trials, channels, forward, inverse):
    beam_count = series.shape[0]
    chan_count = series.shape[1]
    rows = series.reshape(beam_count * chan_count, 2 * FRAMES)
    spectrum = jnp.dot(
        rows, forward, precision=lax.Precision.HIGHEST, preferred_element_type=jnp.float32
    )
    spectrum = spectrum.reshape(beam_count, chan_count, 2, FRAMES)
    measure = (trials + 1).astype(jnp.float32) / NDM
    freq = 1.0 + channels.astype(jnp.float32) / CH
    spread = 1.0 / (freq * freq * freq)
    coeff = math.pi * measure[:, None] * spread[None, :]
    bins = jnp.arange(FRAMES, dtype=jnp.int32)
    kappa = jnp.where(bins < FRAMES // 2, bins, bins - FRAMES).astype(jnp.float32)
    phase = coeff[:, :, None] * (kappa * kappa / FRAMES)[None, None, :]
    cosine = jnp.cos(phase)
    sine = jnp.sin(phase)
    real_part = spectrum[:, :, 0] * cosine - spectrum[:, :, 1] * sine
    imag_part = spectrum[:, :, 0] * sine + spectrum[:, :, 1] * cosine
    rotated = jnp.stack((real_part, imag_part), axis=2).reshape(beam_count * chan_count, 2 * FRAMES)
    result = jnp.dot(
        rotated, inverse, precision=lax.Precision.HIGHEST, preferred_element_type=jnp.float32
    )
    result = result.reshape(beam_count, chan_count, 2, FRAMES)
    return result[:, :, 0] * result[:, :, 0] + result[:, :, 1] * result[:, :, 1]


def body(voltages, station_map, beam_table, weight_table, dm_trial):
    section_index = lax.axis_index("section")
    dom_index = lax.axis_index("dom")
    section_count = lax.axis_size("section")
    dom_count = lax.axis_size("dom")
    local_stations = voltages.shape[0]
    chan_local = weight_table.shape[2]
    per_device = BEAMS // (section_count * dom_count)
    frame_count = FRAMES // section_count
    rows_here = local_stations * frame_count
    block = lax.dynamic_slice_in_dim(voltages, section_index * frame_count, frame_count, 1)
    rows = block.reshape(rows_here, NFFT)
    spectrum = lax.dot_general(
        dft_table(), rows, (((0,), (1,)), ((), ())), preferred_element_type=jnp.float32
    )
    spectrum = spectrum.astype(jnp.bfloat16).reshape(2, CH, rows_here)
    turned = lax.all_to_all(spectrum, "dom", split_axis=1, concat_axis=2, tiled=True)
    signal = turned.reshape(2, chan_local, NSTAT, frame_count)
    arrival = jnp.take(beam_table, station_map, axis=1)
    onehot = (arrival.reshape(-1)[None, :] == jnp.arange(NTAB, dtype=jnp.int32)[:, None]).astype(
        jnp.bfloat16
    )
    mixed = jnp.einsum("rtc,tn->crn", weight_table, onehot, preferred_element_type=jnp.float32)
    weights = mixed.astype(jnp.bfloat16).reshape(chan_local, 2 * BEAMS, NSTAT)
    product = jnp.einsum("cks,rcsf->kcrf", weights, signal, preferred_element_type=jnp.float32)
    beam_re = product[:BEAMS, :, 0] - product[BEAMS:, :, 1]
    beam_im = product[:BEAMS, :, 1] + product[BEAMS:, :, 0]
    beams_now = jnp.stack((beam_re, beam_im), axis=2)
    owned = lax.all_to_all(beams_now, ("section", "dom"), split_axis=0, concat_axis=0, tiled=True)
    series = owned.reshape(section_count, dom_count, per_device, chan_local, 2, frame_count)
    series = series.transpose(2, 1, 3, 4, 0, 5).reshape(per_device, CH, 2, FRAMES)
    owner = section_index * dom_count + dom_index
    trials = lax.dynamic_slice_in_dim(dm_trial, owner * per_device, per_device, 0)
    forward, inverse = frame_tables()
    detected = dedisperse(series, trials, jnp.arange(CH, dtype=jnp.int32), forward, inverse)
    return detected.transpose(0, 2, 1)


def solution(mesh):
    in_specs = (P("dom", None, None), P(), P(), P(None, None, "dom"), P())
    out_specs = P(("section", "dom"), None, None)
    return jax.shard_map(body, mesh=mesh, in_specs=in_specs, out_specs=out_specs, check_vma=False)
```

profile of v0, /device:TPU:1, one launch (start us, length us, event | category | flops | bytes accessed | tf_op | source)
XLA Modules:
  0.0 179.8 jit_solution(3970701460906797980)
XLA Ops:
  0.1 1.3 constant_dynamic-slice_fusion
  1.4 69.8 %fusion.12 = bf16[2048,256]{1,0:T(8,128)(2,1)S(1)} fusion(bf16[256,2048]{1,0:T(8,128)(2,1)S(1)} %bitcast.70, f32[2048]{0:T(1024)S(1)} %subtract_multiply_fusion, s32[2048]{0:T(1024)S(1)} %add_select_fusion.2, pred[2048]{0:T(1024)(128)(4,1)S(1)} %iota_compare_fusion.2), kind=kOutput, calls=%fused_computation.19 | convolution fusion | flops 2223505408 | bytes 2115584 | tf_op jit(solution)/shard_map/dot_general | solution.py:87
  71.3 2.1 %copy.35 = bf16[2,1024,256]{2,0,1:T(2,128)(2,1)} copy(bf16[2,1024,256]{2,1,0:T(8,128)(2,1)S(1)} %bitcast.71) | data formatting | bytes 2097152 | tf_op jit(solution)/shard_map/reshape | solution.py:90
  73.3 10.0 %all-to-all-start = ((bf16[2,1024,256]{2,0,1:T(2,128)(2,1)}), bf16[2,1024,256]{2,0,1:T(2,128)(2,1)S(1)}, u32[]{:S(2)}, u32[]{:S(2)}) async-start(bf16[2,1024,256]{2,0,1:T(2,128)(2,1)} %copy.35), calls=%async_computation | async-start | bytes 2097152 | tf_op jit(solution)/shard_map/all_to_all | solution.py:91
  83.4 0.1 copy.38
  83.5 1.0 gather_fusion
  84.5 0.1 select_bitcast_fusion
  84.7 0.1 copy.39
  84.9 2.6 %fusion.6 = f32[65536,64]{0,1:S(1)} fusion(bf16[64,64]{0,1:T(8,128)(2,1)S(1)} %bitcast.61, s32[65536]{0:T(1024)S(1)} %bitcast.69), kind=kOutput, calls=%fused_computation.12 | convolution fusion | flops 541065216 | bytes 17047552
  87.5 0.9 convert_bitcast_fusion
  88.4 15.6 %copy.40 = bf16[32,2,65536]{2,1,0:T(2,128)(2,1)} copy(bf16[32,2,65536]{2,0,1:T(8,128)(2,1)S(1)} %convert_bitcast_fusion) | data formatting | bytes 16777216 | tf_op jit(solution)/shard_map/convert_element_type | solution.py:98
  104.1 21.6 %reshape.268 = bf16[32,256,512,1]{2,1,0,3:T(8,128)(2,1)} reshape(bf16[32,2,65536]{2,1,0:T(2,128)(2,1)} %copy.40) | data formatting | bytes 16777216 | tf_op jit(solution)/shard_map/reshape | solution.py:98
  125.7 0.6 dynamic_slice.7
  126.9 0.1 copy.36
  127.0 3.2 %copy.37 = bf16[2,32,32,256]{1,3,2,0:T(8,128)(2,1)} copy(bf16[2,32,32,256]{3,1,2,0:T(8,128)(2,1)S(1)} %bitcast.67) | data formatting | bytes 2097152 | tf_op jit(solution)/shard_map/all_to_all | solution.py:91
  130.2 5.2 %copy.41 = bf16[2,32,512,16]{2,3,0,1:T(8,128)(2,1)S(1)} copy(bf16[2,32,512,16]{1,3,2,0:T(8,128)(2,1)} %bitcast.63) | data formatting | bytes 2097152 | tf_op jit(solution)/shard_map/reshape | solution.py:92
  135.5 5.9 %fusion.13 = f32[256,32,2,16]{0,3,2,1:T(8,128)S(1)} fusion(bf16[2,32,512,16]{2,3,0,1:T(8,128)(2,1)S(1)} %copy.41, bf16[32,256,512,1]{2,1,0,3:T(8,128)(2,1)} %reshape.268), kind=kOutput, calls=%fused_computation.21 | convolution fusion | flops 268435456 | bytes 10485760 | tf_op jit(solution)/shard_map/cks,rcsf->kcrf/dot_general | solution.py:99
  141.5 1.9 %copy.42 = f32[128,32,2,16]{1,3,2,0:T(8,128)S(1)} copy(f32[128,32,2,16]{0,3,2,1:T(8,128)S(1)} %pad_maximum_fusion) | data formatting | bytes 1048576 | tf_op jit(solution)/shard_map/stack | solution.py:102
  143.4 1.7 reshape.272
  145.1 9.5 %all-to-all-start.1 = ((f32[128,1,1024]{2,1,0:T(1,128)}), f32[128,1,1024]{2,1,0:T(1,128)S(1)}, u32[]{:S(2)}, u32[]{:S(2)}) async-start(f32[128,1,1024]{2,1,0:T(1,128)} %reshape.272), calls=%async_computation.1 | async-start | bytes 1048576 | tf_op jit(solution)/shard_map/all_to_all | solution.py:103
  154.7 0.1 fusion.36
  154.9 0.1 fusion.34
  155.1 13.4 %all-to-all-done.1 = f32[128,1,1024]{2,1,0:T(1,128)S(1)} async-done(((f32[128,1,1024]{2,1,0:T(1,128)}), f32[128,1,1024]{2,1,0:T(1,128)S(1)}, u32[]{:S(2)}, u32[]{:S(2)}) %all-to-all-start.1) | async-done | bytes 524320 | tf_op jit(solution)/shard_map/all_to_all | solution.py:103
  168.5 0.5 broadcast.225
  169.1 1.9 %reduce = f32[128,1024]{1,0:T(8,128)S(1)} reduce(f32[128,1,1024]{2,1,0:T(1,128)S(1)} %all-to-all-done.1, f32[]{:T(128)} %broadcast.225), dimensions={1}, to_apply=%all_to_all.17.reduce_sub_computation | reduce | bytes 1048580 | tf_op jit(solution)/shard_map/all_to_all | solution.py:103
  170.9 0.7 reshape.273
  171.6 2.6 %copy.53 = f32[4,32,1,32,2,16]{3,1,5,0,4,2:T(8,128)} copy(f32[4,32,1,32,2,16]{3,5,4,1,0,2:T(8,128)S(1)} %bitcast.65) | data formatting | bytes 1048576 | tf_op jit(solution)/shard_map/reshape | solution.py:104
  174.2 2.4 %reshape.255 = f32[1024,128]{0,1:T(8,128)S(1)} reshape(f32[1,32,32,2,4,16]{2,1,5,4,3,0:T(8,128)} %bitcast.66) | data formatting | bytes 1048576 | tf_op jit(solution)/shard_map/reshape.74
  176.6 0.6 convolution_bitcast_fusion.1
  177.2 1.2 fusion.21
  178.5 0.6 convolution_bitcast_fusion
  179.1 0.7 fusion.24
  (22 shorter events, 0.4 us)
Async XLA Ops:
  0.0 84.9 %copy-start = (bf16[2,64,32]{1,2,0:T(8,128)(2,1)S(1)}, bf16[2,64,32]{1,2,0:T(8,128)(2,1)}, u32[]{:S(2)}) copy-start(bf16[2,64,32]{1,2,0:T(8,128)(2,1)} %param.8) | copy-start | bytes 24580
  1.4 81.9 %copy-start.2 = (s32[512]{0:T(512)S(1)}, s32[512]{0:T(512)}, u32[]{:S(2)}) copy-start(s32[512]{0:T(512)} %param.6) | copy-start | bytes 6148
  1.4 82.0 %copy-start.1 = (s32[128,512]{1,0:T(8,128)S(1)}, s32[128,512]{1,0:T(8,128)}, u32[]{:S(2)}) copy-start(s32[128,512]{1,0:T(8,128)} %param.7) | copy-start | bytes 786436
  73.3 53.6 %all-to-all-start = ((bf16[2,1024,256]{2,0,1:T(2,128)(2,1)}), bf16[2,1024,256]{2,0,1:T(2,128)(2,1)S(1)}, u32[]{:S(2)}, u32[]{:S(2)}) async-start(bf16[2,1024,256]{2,0,1:T(2,128)(2,1)} %copy.35), calls=%async_computation | async-start | bytes 2097152 | tf_op jit(solution)/shard_map/all_to_all | solution.py:91
  88.4 37.2 %copy-start.3 = (s32[128]{0:T(128)S(1)}, s32[128]{0:T(128)}, u32[]{:S(2)}) copy-start(s32[128]{0:T(128)} %param.9) | copy-start | bytes 1540
  145.1 23.4 %all-to-all-start.1 = ((f32[128,1,1024]{2,1,0:T(1,128)}), f32[128,1,1024]{2,1,0:T(1,128)S(1)}, u32[]{:S(2)}, u32[]{:S(2)}) async-start(f32[128,1,1024]{2,1,0:T(1,128)} %reshape.272), calls=%async_computation.1 | async-start | bytes 1048576 | tf_op jit(solution)/shard_map/all_to_all | solution.py:103
where the time goes:
time: 181 us; the launch traced here: 180 us
  matrix products  79.5 us (44%)
  local copies, waits for them, and re-layouts  60.9 us (34%)
  starting transfers between devices  19.5 us (11%)
  waiting for transfers between devices  13.4 us (7%)
  other arithmetic  5.45 us (3%)
    dot_general x1, matrix products, body(): lax.dot_general(dft_table(), rows, (((0,), (1,)), ((), ())), preferred_el...  69.8 us
    reshape x1, local copies, waits for them, and re-layouts, body(): weights = mixed.astype(jnp.bfloat16).reshape(chan_local, 2 * BEAMS, NSTAT)  21.6 us
    convert_element_type x1, local copies, waits for them, and re-layouts, body(): weights = mixed.astype(jnp.bfloat16).reshape(chan_local, 2 * BEAMS, NSTAT)  15.6 us
    all_to_all x1, waiting for transfers between devices, body(): lax.all_to_all(beams_now, ('section', 'dom'), split_axis=0, concat_axis=0...  13.4 us
    all_to_all x1, starting transfers between devices, body(): lax.all_to_all(spectrum, 'dom', split_axis=1, concat_axis=2, tiled=True)  9.99 us
    all_to_all x1, starting transfers between devices, body(): lax.all_to_all(beams_now, ('section', 'dom'), split_axis=0, concat_axis=0...  9.54 us
    dot_general x1, matrix products, body(): jnp.einsum('cks,rcsf->kcrf', weights, signal, preferred_element_type=jnp....  5.91 us
    reshape x1, local copies, waits for them, and re-layouts, body(): signal = turned.reshape(2, chan_local, NSTAT, frame_count)  5.24 us
  transfers between devices with their start and end apart: 2, of which 1 were waited for; matrix products, arithmetic and copies ran while one was open for 24% of the time, Pallas kernels for 0%

commit v1 on v0

v1 whole, which is shorter than its diff:
```python
import math

import jax
import jax.numpy as jnp
import ml_dtypes
import numpy as np
from jax import lax
from jax.experimental import pallas as pl
from jax.experimental.pallas import tpu as pltpu
from jax.sharding import PartitionSpec as P

NSTAT = 512
NFFT = 2048
CH = 1024
BEAMS = 128
NTAB = 64
FRAMES = 64
NDM = 32
SECTIONS = 4
DOMS = 32
STATIONS = NSTAT // DOMS
MINE = CH // (SECTIONS * DOMS)
LANES = 128
COLS = 2 * CH // SECTIONS
STEPS = 4
NT = (((1,), (1,)), ((), ()))
F32 = jnp.float32
BF16 = jnp.bfloat16


def dft_table():
    sample = np.arange(NFFT)
    window = 0.5 - 0.5 * np.cos(sample.astype(np.float32) * np.float32(2.0 * math.pi / NFFT))
    scale = (window / np.float32(math.sqrt(NFFT))).astype(np.float32)
    angle = (np.arange(CH)[:, None] * sample[None, :] % NFFT).astype(np.float32) * np.float32(
        2.0 * math.pi / NFFT
    )
    parts = np.stack((np.cos(angle) * scale, -np.sin(angle) * scale))
    parts = parts.reshape(2, DOMS, SECTIONS, MINE, NFFT).transpose(2, 1, 0, 3, 4)
    return parts.reshape(SECTIONS, COLS, NFFT).astype(ml_dtypes.bfloat16)


def frame_tables():
    index = np.arange(FRAMES)
    angle = (index[:, None] * index[None, :] % FRAMES) * (2.0 * math.pi / FRAMES)
    cosine, sine = np.cos(angle), np.sin(angle)
    forward = np.block([[cosine, -sine], [sine, cosine]])
    inverse = np.block([[cosine, sine], [-sine, cosine]]) / FRAMES
    tables = []
    for table in (forward, inverse):
        high = table.astype(ml_dtypes.bfloat16)
        tables += [high, (table - high.astype(np.float64)).astype(ml_dtypes.bfloat16)]
    return np.stack(tables)


def channelise_kernel(table_hbm, volts_hbm, out_ref, table, volts, turned, table_sem, volts_sem):
    section = lax.axis_index("section")
    share = STATIONS * FRAMES // STEPS
    get_table = pltpu.make_async_copy(table_hbm.at[section], table, table_sem)
    get_volts = [
        pltpu.make_async_copy(
            volts_hbm.at[pl.ds(n * share, share)], volts.at[n], volts_sem.at[n]
        )
        for n in range(STEPS)
    ]
    get_volts[0].start()
    get_table.start()
    for n in range(1, STEPS):
        get_volts[n].start()
    get_table.wait()
    low = lax.broadcasted_iota(jnp.int32, (8, LANES), 1) < FRAMES
    for n in range(STEPS):
        get_volts[n].wait()
        spectrum = lax.dot_general(table[...], volts[n], NT, preferred_element_type=F32)
        for d in range(DOMS):
            for t in range(share // LANES):
                real = spectrum[16 * d : 16 * d + 8, LANES * t : LANES * (t + 1)]
                imag = spectrum[16 * d + 8 : 16 * d + 16, LANES * t : LANES * (t + 1)]
                station = (n * share + t * LANES) // FRAMES
                base = d * MINE * STATIONS + station
                turned[pl.ds(base, 8, stride=STATIONS), :] = jnp.where(
                    low, real, pltpu.roll(imag, FRAMES, 1)
                )
                turned[pl.ds(base + 1, 8, stride=STATIONS), :] = jnp.where(
                    low, pltpu.roll(real, FRAMES, 1), imag
                )
    for d in range(DOMS):
        out_ref[d] = turned[pl.ds(d * LANES, LANES), :].astype(BF16)


def channelise(table, volts):
    return pl.pallas_call(
        channelise_kernel,
        name="channelise",
        out_shape=jax.ShapeDtypeStruct((DOMS, MINE * STATIONS, LANES), BF16),
        in_specs=[pl.BlockSpec(memory_space=pl.ANY)] * 2,
        out_specs=pl.BlockSpec(memory_space=pltpu.VMEM),
        scratch_shapes=[
            pltpu.VMEM((COLS, NFFT), BF16),
            pltpu.VMEM((STEPS, STATIONS * FRAMES // STEPS, NFFT), BF16),
            pltpu.VMEM((DOMS * MINE * STATIONS, LANES), F32),
            pltpu.SemaphoreType.DMA,
            pltpu.SemaphoreType.DMA((STEPS,)),
        ],
        compiler_params=pltpu.CompilerParams(vmem_limit_bytes=32 << 20),
        cost_estimate=pl.CostEstimate(
            flops=2 * COLS * NFFT * STATIONS * FRAMES, bytes_accessed=7 << 20, transcendentals=0
        ),
    )(table, volts)


def prep_kernel(map_ref, beam_ref, weight_ref, trial_ref, out_ref, turn_ref):
    section, dom = lax.axis_index("section"), lax.axis_index("dom")
    station = lax.broadcasted_iota(jnp.int32, (NSTAT, NSTAT), 0)
    chosen = jnp.where(station == map_ref[...], 1.0, 0.0).astype(BF16)
    entries = jnp.dot(
        beam_ref[...].astype(F32).astype(BF16), chosen, preferred_element_type=F32
    ).astype(jnp.int32)
    here = lax.broadcasted_iota(jnp.int32, (MINE, DOMS), 1)
    wanted = lax.broadcasted_iota(jnp.int32, (MINE, DOMS), 0) + section * MINE
    select = jnp.where(here == wanted, 1.0, 0.0).astype(BF16)
    weights = lax.dot_general(select, weight_ref[...], NT, preferred_element_type=F32)
    for j in range(MINE):
        row = jnp.broadcast_to(weights[j : j + 1, :], (BEAMS, LANES))
        for part in range(2):
            for t in range(NSTAT // LANES):
                which = entries[:, LANES * t : LANES * (t + 1)] + part * NTAB
                value = jnp.take_along_axis(row, which, axis=1)
                out_ref[j, pl.ds(part * BEAMS, BEAMS), pl.ds(LANES * t, LANES)] = value.astype(BF16)
    trial = lax.broadcasted_iota(jnp.int32, (NDM, LANES), 0)
    lane = lax.broadcasted_iota(jnp.int32, (NDM, LANES), 1)
    k = lane % FRAMES
    kappa = jnp.where(k < FRAMES // 2, k, k - FRAMES).astype(F32)
    measure = (trial + 1).astype(F32) / NDM
    column = jnp.broadcast_to(trial_ref[...].astype(F32), (BEAMS, BEAMS)).T
    onehot = jnp.where(
        column[:, :NDM] == lax.broadcasted_iota(jnp.int32, (BEAMS, NDM), 1).astype(F32), 1.0, 0.0
    )
    for j in range(MINE):
        channel = jnp.full((NDM, LANES), dom * (SECTIONS * MINE) + section * MINE + j, jnp.int32)
        freq = 1.0 + channel.astype(F32) / CH
        spread = 1.0 / (freq * freq * freq)
        phase = math.pi * measure * spread * (kappa * kappa / FRAMES)
        sine = jnp.sin(phase)
        turn_ref[0, j] = jnp.dot(
            onehot, jnp.cos(phase), precision=lax.Precision.HIGHEST, preferred_element_type=F32
        )
        turn_ref[1, j] = jnp.dot(
            onehot,
            jnp.where(lane < FRAMES, -sine, sine),
            precision=lax.Precision.HIGHEST,
            preferred_element_type=F32,
        )


def prep(station_map, beam_table, weight_table, dm_trial):
    return pl.pallas_call(
        prep_kernel,
        name="prep",
        out_shape=(
            jax.ShapeDtypeStruct((MINE, 2 * BEAMS, NSTAT), BF16),
            jax.ShapeDtypeStruct((2, MINE, BEAMS, LANES), F32),
        ),
        compiler_params=pltpu.CompilerParams(vmem_limit_bytes=32 << 20),
        cost_estimate=pl.CostEstimate(
            flops=4_000_000_000, bytes_accessed=16 << 20, transcendentals=65536
        ),
    )(
        station_map.reshape(1, NSTAT),
        beam_table,
        weight_table.reshape(2 * NTAB, weight_table.shape[2]),
        dm_trial.reshape(1, BEAMS),
    )


def split_dot(rows, high, low):
    top = rows.astype(BF16)
    rest = (rows - top.astype(F32)).astype(BF16)
    return (
        jnp.dot(top, high, preferred_element_type=F32)
        + jnp.dot(rest, high, preferred_element_type=F32)
        + jnp.dot(top, low, preferred_element_type=F32)
    )


def beam_kernel(
    signal_hbm, weight_hbm, turn_hbm, frame_ref, out_ref, signal, weight, turn, power, sems
):
    copies = []
    for j in range(MINE):
        rows = pl.ds(j * STATIONS, STATIONS)
        copies.append(
            (
                pltpu.make_async_copy(signal_hbm.at[:, rows], signal.at[j], sems.at[j, 0]),
                pltpu.make_async_copy(weight_hbm.at[j], weight.at[j], sems.at[j, 1]),
                pltpu.make_async_copy(turn_hbm.at[:, j], turn.at[j], sems.at[j, 2]),
            )
        )
    for group in copies:
        for copy in group:
            copy.start()
    low = lax.broadcasted_iota(jnp.int32, (BEAMS, LANES), 1) < FRAMES
    half = MINE // 2
    for q in range(half):
        found = []
        for j in (q, q + half):
            for copy in copies[j]:
                copy.wait()
            product = jnp.dot(
                weight[j], signal[j].reshape(NSTAT, LANES), preferred_element_type=F32
            )
            crossed = pltpu.roll(product[BEAMS:], FRAMES, 1)
            series = product[:BEAMS] + jnp.where(low, -crossed, crossed)
            bins = split_dot(series, frame_ref[0], frame_ref[1])
            rotated = bins * turn[j, 0] + pltpu.roll(bins, FRAMES, 1) * turn[j, 1]
            result = split_dot(rotated, frame_ref[2], frame_ref[3])
            square = result * result
            found.append(square + pltpu.roll(square, FRAMES, 1))
        power[pl.ds(q, BEAMS, stride=half), :] = jnp.where(low, found[0], found[1])
    out_ref[...] = power[...].astype(BF16)


def form_beams(signal, weights, turns, frames):
    return pl.pallas_call(
        beam_kernel,
        name="beams",
        out_shape=jax.ShapeDtypeStruct((BEAMS * MINE // 2, LANES), BF16),
        in_specs=[pl.BlockSpec(memory_space=pl.ANY)] * 3 + [pl.BlockSpec(memory_space=pltpu.VMEM)],
        out_specs=pl.BlockSpec(memory_space=pltpu.VMEM),
        scratch_shapes=[
            pltpu.VMEM((MINE, DOMS, STATIONS, LANES), BF16),
            pltpu.VMEM((MINE, 2 * BEAMS, NSTAT), BF16),
            pltpu.VMEM((MINE, 2, BEAMS, LANES), F32),
            pltpu.VMEM((BEAMS * MINE // 2, LANES), F32),
            pltpu.SemaphoreType.DMA((MINE, 3)),
        ],
        compiler_params=pltpu.CompilerParams(vmem_limit_bytes=32 << 20),
        cost_estimate=pl.CostEstimate(
            flops=400_000_000, bytes_accessed=4 << 20, transcendentals=0
        ),
    )(signal, weights, turns, frames)


def order_kernel(power_ref, out_ref):
    half = MINE // 2
    count = SECTIONS * DOMS * half
    channel = lax.broadcasted_iota(jnp.int32, (count, CH), 1)
    row = lax.broadcasted_iota(jnp.int32, (count, CH), 0)
    owner = channel // (SECTIONS * MINE)
    section = channel // MINE % SECTIONS
    wanted = section * (DOMS * half) + owner * half + channel % half
    place = jnp.where(row == wanted, 1.0, 0.0).astype(BF16)
    turned = power_ref[...].astype(F32).T.astype(BF16)
    placed = jnp.dot(turned, place, preferred_element_type=F32)
    high = lax.broadcasted_iota(jnp.int32, (FRAMES, CH), 1) // half % 2 == 1
    out_ref[0] = jnp.where(high, placed[FRAMES:], placed[:FRAMES])


def order(power):
    return pl.pallas_call(
        order_kernel,
        name="order",
        out_shape=jax.ShapeDtypeStruct((1, FRAMES, CH), F32),
        compiler_params=pltpu.CompilerParams(vmem_limit_bytes=32 << 20),
    )(power)


def body(voltages, station_map, beam_table, weight_table, dm_trial):
    volts = voltages.reshape(STATIONS * FRAMES, NFFT)
    spectra = channelise(jnp.asarray(dft_table()), volts)
    signal = lax.all_to_all(spectra, "dom", split_axis=0, concat_axis=0, tiled=True)
    weights, turns = prep(station_map, beam_table, weight_table, dm_trial)
    power = form_beams(signal, weights, turns, jnp.asarray(frame_tables()))
    power = power.reshape(BEAMS, MINE // 2, LANES)
    power = lax.all_to_all(power, ("section", "dom"), split_axis=0, concat_axis=0, tiled=True)
    return order(power.reshape(BEAMS * MINE // 2, LANES))


def solution(mesh):
    in_specs = (P("dom", None, None), P(), P(), P(None, None, "dom"), P())
    out_specs = P(("section", "dom"), None, None)
    return jax.shard_map(body, mesh=mesh, in_specs=in_specs, out_specs=out_specs, check_vma=False)
```

time: 181 us -> 65.9 us (0.36)
  matrix products: 79.5 us -> 0 us
  local copies, waits for them, and re-layouts: 60.9 us -> 8.86 us
  Pallas kernels: 0 us -> 17.2 us
  blocking collectives: 0 us -> 16.9 us
  starting transfers between devices: 19.5 us -> 9.82 us
  other arithmetic: 5.45 us -> 0 us
    dot_general x4 -> x0, matrix products: 76.9 us -> none  [the longest x1 69.8 us: body(): lax.dot_general(dft_table(), rows, (((0,), (1,)), ((), ())), preferred_el...]
    reshape x4 -> x0, local copies, waits for them, and re-layouts: 31.4 us -> none  [the longest x1 21.6 us: body(): weights = mixed.astype(jnp.bfloat16).reshape(chan_local, 2 * BEAMS, NSTAT)]
    pallas_call x0 -> x4, Pallas kernels: none -> 17.2 us  [the longest x1 7.13 us: form_beams(): pl.pallas_call(beam_kernel, name='beams', out_shape=jax.ShapeDtypeStruct(...]
    all_to_all x0 -> x1, blocking collectives: none -> 16.9 us  [body(): lax.all_to_all(power, ('section', 'dom'), split_axis=0, concat_axis=0, ti...]
    convert_element_type x1 -> x0, local copies, waits for them, and re-layouts: 15.6 us -> none  [body(): weights = mixed.astype(jnp.bfloat16).reshape(chan_local, 2 * BEAMS, NSTAT)]
    all_to_all x2 -> x1, starting transfers between devices: 19.5 us -> 9.82 us  [body(): lax.all_to_all(spectra, 'dom', split_axis=0, concat_axis=0, tiled=True)]
    unnamed x12 -> x19, local copies, waits for them, and re-layouts: 2.62 us -> 8.86 us
    another operation x2 -> x0, local copies, waits for them, and re-layouts: 4.32 us -> none
  transfers between devices with their start and end apart: 2 -> 1, of which waited for: 1 -> 1; matrix products, arithmetic and copies ran while one was open for 24% -> 0% of each run, Pallas kernels for 0% -> 3%
where the time goes in v1:
time: 65.9 us; the launch traced here: 65.5 us
  Pallas kernels  17.2 us (26%)
  blocking collectives  16.9 us (26%)
  waiting for transfers between devices  12.7 us (19%)
  starting transfers between devices  9.82 us (15%)
  local copies, waits for them, and re-layouts  8.86 us (13%)
    all_to_all x1, blocking collectives, body(): lax.all_to_all(power, ('section', 'dom'), split_axis=0, concat_axis=0, ti...  16.9 us
    all_to_all x1, waiting for transfers between devices, body(): lax.all_to_all(spectra, 'dom', split_axis=0, concat_axis=0, tiled=True)  12.7 us
    all_to_all x1, starting transfers between devices, body(): lax.all_to_all(spectra, 'dom', split_axis=0, concat_axis=0, tiled=True)  9.82 us
    unnamed x19, local copies, waits for them, and re-layouts  8.86 us
    pallas_call x1, Pallas kernels, form_beams(): pl.pallas_call(beam_kernel, name='beams', out_shape=jax.ShapeDtypeStruct(...  7.13 us
    pallas_call x1, Pallas kernels, channelise(): pl.pallas_call(channelise_kernel, name='channelise', out_shape=jax.ShapeD...  6.94 us
    pallas_call x1, Pallas kernels, prep(): pl.pallas_call(prep_kernel, name='prep', out_shape=(jax.ShapeDtypeStruct(...  1.96 us
  transfers between devices with their start and end apart: 1, of which 1 were waited for; matrix products, arithmetic and copies ran while one was open for 0% of the time, Pallas kernels for 3%

profile of v1, /device:TPU:1, one launch (start us, length us, event | category | flops | bytes accessed | tf_op | source)
XLA Modules:
  0.0 65.5 jit_solution(14759430849900397555)
XLA Ops:
  0.0 0.0 copy-start
  0.0 3.4 %copy-done = bf16[4,512,2048]{2,1,0:T(8,128)(2,1)S(1)} copy-done((bf16[4,512,2048]{2,1,0:T(8,128)(2,1)S(1)}, bf16[4,512,2048]{2,1,0:T(8,128)(2,1)}, u32[]{:S(2)}) %copy-start) | copy-done | bytes 8388632
  3.4 0.0 copy-start.1
  3.4 2.2 %copy-done.1 = bf16[16,64,2048]{2,1,0:T(8,128)(2,1)S(1)} copy-done((bf16[16,64,2048]{2,1,0:T(8,128)(2,1)S(1)}, bf16[16,64,2048]{2,1,0:T(8,128)(2,1)}, u32[]{:S(2)}) %copy-start.1) | copy-done | bytes 4194328
  5.6 0.0 copy-start.8
  5.6 0.0 copy-start.6
  5.6 0.0 copy-start.7
  5.6 6.9 %channelise.1 = bf16[32,128,128]{2,1,0:T(8,128)(2,1)} custom-call(bf16[4,512,2048]{2,1,0:T(8,128)(2,1)S(1)} %copy-done, bf16[1024,2048]{1,0:T(8,128)(2,1)S(1)} %bitcast.6), custom_call_target="tpu_custom_call" | custom-call | flops 2147483648 | bytes 7340032 | tf_op jit(solution)/shard_map/channelise/pallas_call | solution.py:92
  12.5 9.8 %all-to-all-start = ((bf16[32,128,128]{2,1,0:T(8,128)(2,1)}), bf16[32,128,128]{2,1,0:T(8,128)(2,1)S(1)}, u32[]{:S(2)}, u32[]{:S(2)}) async-start(bf16[32,128,128]{2,1,0:T(8,128)(2,1)} %channelise.1), calls=%async_computation | async-start | bytes 2097152 | tf_op jit(solution)/shard_map/all_to_all | solution.py:271
  22.4 0.0 copy-done.8
  22.4 0.1 copy.8
  22.5 0.0 copy-done.6
  22.5 0.0 copy-done.7
  22.5 0.0 copy-start.5
  22.5 0.9 %copy-done.5 = s32[128,512]{1,0:T(8,128)S(1)} copy-done((s32[128,512]{1,0:T(8,128)S(1)}, s32[128,512]{1,0:T(8,128)}, u32[]{:S(2)}) %copy-start.5) | copy-done | bytes 262168
  23.4 0.0 copy-start.4
  23.4 2.0 %prep.1 = (bf16[8,256,512]{2,1,0:T(8,128)(2,1)S(1)}, f32[2,8,128,128]{3,2,1,0:T(8,128)S(1)}) custom-call(s32[1,512]{1,0:T(1,128)S(1)} %bitcast.10, s32[128,512]{1,0:T(8,128)S(1)} %copy-done.5, bf16[128,32]{1,0:T(8,128)(2,1)S(1)} %bitcast.9, s32[1,128]{1,0:T(1,128)S(1)} %bitcast.11), custom_call_target="tpu_custom_call" | custom-call | flops 4000000000 | bytes 16777216 | tf_op jit(solution)/shard_map/prep/pallas_call | solution.py:157
  25.4 0.0 copy-start.2
  25.4 1.0 %copy-done.2 = f32[2,8,128,128]{3,2,1,0:T(8,128)} copy-done((f32[2,8,128,128]{3,2,1,0:T(8,128)}, f32[2,8,128,128]{3,2,1,0:T(8,128)S(1)}, u32[]{:S(2)}) %copy-start.2) | copy-done | bytes 1048600
  26.4 12.7 %all-to-all-done.signal_hbm = bf16[32,128,128]{2,1,0:T(8,128)(2,1)S(1)} async-done(((bf16[32,128,128]{2,1,0:T(8,128)(2,1)}), bf16[32,128,128]{2,1,0:T(8,128)(2,1)S(1)}, u32[]{:S(2)}, u32[]{:S(2)}) %all-to-all-start) | async-done | bytes 1048608 | tf_op jit(solution)/shard_map/all_to_all | solution.py:271
  39.1 0.0 copy-done.4
  39.1 0.0 copy-start.3
  39.1 1.2 %copy-done.3 = f32[2,8,128,128]{3,2,1,0:T(8,128)S(1)} copy-done((f32[2,8,128,128]{3,2,1,0:T(8,128)S(1)}, f32[2,8,128,128]{3,2,1,0:T(8,128)}, u32[]{:S(2)}) %copy-start.3) | copy-done | bytes 1048600
  40.3 7.1 %beams.1 = bf16[512,128]{1,0:T(8,128)(2,1)S(1)} custom-call(bf16[32,128,128]{2,1,0:T(8,128)(2,1)S(1)} %all-to-all-done.signal_hbm, bf16[8,256,512]{2,1,0:T(8,128)(2,1)S(1)} %get-tuple-element.7.weight_hbm, f32[2,8,128,128]{3,2,1,0:T(8,128)S(1)} %copy-done.3, bf16[4,128,128]{2,1,0:T(8,128)(2,1)S(1)} %copy-done.4), custom_call_target="tpu_custom_call" | custom-call | flops 400000000 | bytes 4194304 | tf_op jit(solution)/shard_map/beams/pallas_call | solution.py:224
  47.4 16.9 %all_to_all.10 = bf16[128,4,128]{2,1,0:T(4,128)(2,1)S(1)} all-to-all(bf16[128,4,128]{2,1,0:T(4,128)(2,1)S(1)} %bitcast.7), channel_id=1, replica_groups=mesh['section'=4,'dom'=32] {'section','dom'}, dimensions={0} | all-to-all | bytes 262144 | tf_op jit(solution)/shard_map/all_to_all | solution.py:275
  64.4 1.1 %order.1 = f32[1,64,1024]{2,1,0:T(8,128)} custom-call(bf16[512,128]{1,0:T(8,128)(2,1)S(1)} %bitcast.8), custom_call_target="tpu_custom_call" | custom-call | tf_op jit(solution)/shard_map/order/pallas_call | solution.py:260
Async XLA Ops:
  0.0 3.4 %copy-start = (bf16[4,512,2048]{2,1,0:T(8,128)(2,1)S(1)}, bf16[4,512,2048]{2,1,0:T(8,128)(2,1)}, u32[]{:S(2)}) copy-start(bf16[4,512,2048]{2,1,0:T(8,128)(2,1)} %constant.4.clone.table_hbm) | copy-start | bytes 25165828
  3.4 2.2 %copy-start.1 = (bf16[16,64,2048]{2,1,0:T(8,128)(2,1)S(1)}, bf16[16,64,2048]{2,1,0:T(8,128)(2,1)}, u32[]{:S(2)}) copy-start(bf16[16,64,2048]{2,1,0:T(8,128)(2,1)} %param.7) | copy-start | bytes 12582916
  5.6 16.8 %copy-start.8 = (bf16[2,64,32]{1,2,0:T(8,128)(2,1)S(1)}, bf16[2,64,32]{1,2,0:T(8,128)(2,1)}, u32[]{:S(2)}) copy-start(bf16[2,64,32]{1,2,0:T(8,128)(2,1)} %param.10) | copy-start | bytes 24580
  5.6 16.9 %copy-start.6 = (s32[512]{0:T(512)S(1)}, s32[512]{0:T(512)}, u32[]{:S(2)}) copy-start(s32[512]{0:T(512)} %param.8) | copy-start | bytes 6148
  5.6 16.9 %copy-start.7 = (s32[128]{0:T(128)S(1)}, s32[128]{0:T(128)}, u32[]{:S(2)}) copy-start(s32[128]{0:T(128)} %param.11) | copy-start | bytes 1540
  12.5 26.6 %all-to-all-start = ((bf16[32,128,128]{2,1,0:T(8,128)(2,1)}), bf16[32,128,128]{2,1,0:T(8,128)(2,1)S(1)}, u32[]{:S(2)}, u32[]{:S(2)}) async-start(bf16[32,128,128]{2,1,0:T(8,128)(2,1)} %channelise.1), calls=%async_computation | async-start | bytes 2097152 | tf_op jit(solution)/shard_map/all_to_all | solution.py:271
  22.5 1.0 %copy-start.5 = (s32[128,512]{1,0:T(8,128)S(1)}, s32[128,512]{1,0:T(8,128)}, u32[]{:S(2)}) copy-start(s32[128,512]{1,0:T(8,128)} %beam_ref.1) | copy-start | bytes 786436
  23.4 15.6 %copy-start.4 = (bf16[4,128,128]{2,1,0:T(8,128)(2,1)S(1)}, bf16[4,128,128]{2,1,0:T(8,128)(2,1)}, u32[]{:S(2)}) copy-start(bf16[4,128,128]{2,1,0:T(8,128)(2,1)} %constant.5.clone.frame_ref) | copy-start | bytes 393220
  25.4 1.0 %copy-start.2 = (f32[2,8,128,128]{3,2,1,0:T(8,128)}, f32[2,8,128,128]{3,2,1,0:T(8,128)S(1)}, u32[]{:S(2)}) copy-start(f32[2,8,128,128]{3,2,1,0:T(8,128)S(1)} %get-tuple-element.8.turn_hbm) | copy-start | bytes 3145732
  39.1 1.2 %copy-start.3 = (f32[2,8,128,128]{3,2,1,0:T(8,128)S(1)}, f32[2,8,128,128]{3,2,1,0:T(8,128)}, u32[]{:S(2)}) copy-start(f32[2,8,128,128]{3,2,1,0:T(8,128)} %copy-done.2) | copy-start | bytes 3145732

commit v2 on v1

v2 whole, which is shorter than its diff:
```python
import math

import jax
import jax.numpy as jnp
import ml_dtypes
import numpy as np
from jax import lax
from jax.experimental import pallas as pl
from jax.experimental.pallas import tpu as pltpu
from jax.sharding import PartitionSpec as P

NSTAT = 512
NFFT = 2048
CH = 1024
BEAMS = 128
NTAB = 64
FRAMES = 64
NDM = 32
SECTIONS = 4
DOMS = 32
STATIONS = NSTAT // DOMS
MINE = CH // (SECTIONS * DOMS)
LANES = 128
COLS = 2 * CH // SECTIONS
STEPS = 4
PIECE = NFFT // STEPS
NT = (((1,), (1,)), ((), ()))
F32 = jnp.float32
BF16 = jnp.bfloat16


def dft_table():
    sample = np.arange(NFFT)
    window = 0.5 - 0.5 * np.cos(sample.astype(np.float32) * np.float32(2.0 * math.pi / NFFT))
    scale = (window / np.float32(math.sqrt(NFFT))).astype(np.float32)
    angle = (np.arange(CH)[:, None] * sample[None, :] % NFFT).astype(np.float32) * np.float32(
        2.0 * math.pi / NFFT
    )
    parts = np.stack((np.cos(angle) * scale, -np.sin(angle) * scale))
    parts = parts.reshape(2, DOMS, SECTIONS, MINE, NFFT).transpose(2, 1, 0, 3, 4)
    return parts.reshape(SECTIONS, COLS, NFFT).astype(ml_dtypes.bfloat16)


def frame_tables():
    index = np.arange(FRAMES)
    angle = (index[:, None] * index[None, :] % FRAMES) * (2.0 * math.pi / FRAMES)
    cosine, sine = np.cos(angle), np.sin(angle)
    forward = np.block([[cosine, -sine], [sine, cosine]])
    inverse = np.block([[cosine, sine], [-sine, cosine]]) / FRAMES
    tables = []
    for table in (forward, inverse):
        high = table.astype(ml_dtypes.bfloat16)
        tables += [high, (table - high.astype(np.float64)).astype(ml_dtypes.bfloat16)]
    return np.stack(tables)


def channelise_kernel(
    table_hbm, volts_hbm, out_hbm, table, volts, total, turned, out, table_sem, volts_sem, out_sem
):
    section = lax.axis_index("section")
    pieces = [pl.ds(n * PIECE, PIECE) for n in range(STEPS)]
    loads = [
        (
            pltpu.make_async_copy(table_hbm.at[section, :, p], table.at[:, p], table_sem.at[n]),
            pltpu.make_async_copy(volts_hbm.at[:, p], volts.at[:, p], volts_sem.at[n]),
        )
        for n, p in enumerate(pieces)
    ]
    for pair in loads:
        for load in pair:
            load.start()
    for n in range(STEPS - 1):
        for load in loads[n]:
            load.wait()
        term = lax.dot_general(
            table[:, pieces[n]], volts[:, pieces[n]], NT, preferred_element_type=F32
        )
        if n == 0:
            total[...] = term
        else:
            total[...] += term
    for load in loads[-1]:
        load.wait()
    low = lax.broadcasted_iota(jnp.int32, (8, LANES), 1) < FRAMES
    for part in range(2):
        rows = pl.ds(part * COLS // 2, COLS // 2)
        spectrum = total[rows, :] + lax.dot_general(
            table[rows, pieces[-1]], volts[:, pieces[-1]], NT, preferred_element_type=F32
        )
        for d in range(DOMS // 2):
            for t in range(STATIONS // 2):
                real = spectrum[16 * d : 16 * d + 8, LANES * t : LANES * (t + 1)]
                imag = spectrum[16 * d + 8 : 16 * d + 16, LANES * t : LANES * (t + 1)]
                base = (part * DOMS // 2 + d) * MINE * STATIONS + 2 * t
                turned[pl.ds(base, 8, stride=STATIONS), :] = jnp.where(
                    low, real, pltpu.roll(imag, FRAMES, 1)
                )
                turned[pl.ds(base + 1, 8, stride=STATIONS), :] = jnp.where(
                    low, pltpu.roll(real, FRAMES, 1), imag
                )
    stores = []
    for part in range(2):
        half = pl.ds(part * DOMS // 2, DOMS // 2)
        for d in range(part * DOMS // 2, (part + 1) * DOMS // 2):
            out[d] = turned[pl.ds(d * LANES, LANES), :].astype(BF16)
        stores.append(pltpu.make_async_copy(out.at[half], out_hbm.at[half], out_sem.at[part]))
        stores[-1].start()
    for store in stores:
        store.wait()


def channelise(table, volts):
    return pl.pallas_call(
        channelise_kernel,
        name="channelise",
        out_shape=jax.ShapeDtypeStruct((DOMS, MINE * STATIONS, LANES), BF16),
        in_specs=[pl.BlockSpec(memory_space=pl.ANY)] * 2,
        out_specs=pl.BlockSpec(memory_space=pl.ANY),
        scratch_shapes=[
            pltpu.VMEM((COLS, NFFT), BF16),
            pltpu.VMEM((STATIONS * FRAMES, NFFT), BF16),
            pltpu.VMEM((COLS, STATIONS * FRAMES), F32),
            pltpu.VMEM((DOMS * MINE * STATIONS, LANES), F32),
            pltpu.VMEM((DOMS, MINE * STATIONS, LANES), BF16),
            pltpu.SemaphoreType.DMA((STEPS,)),
            pltpu.SemaphoreType.DMA((STEPS,)),
            pltpu.SemaphoreType.DMA((2,)),
        ],
        compiler_params=pltpu.CompilerParams(vmem_limit_bytes=61 << 20),
        cost_estimate=pl.CostEstimate(
            flops=2 * COLS * NFFT * STATIONS * FRAMES, bytes_accessed=7 << 20, transcendentals=0
        ),
    )(table, volts)


def prep_kernel(map_ref, beam_ref, weight_ref, out_ref, turn_ref):
    section, dom = lax.axis_index("section"), lax.axis_index("dom")
    station = lax.broadcasted_iota(jnp.int32, (NSTAT, NSTAT), 0)
    chosen = jnp.where(station == map_ref[...], 1.0, 0.0).astype(BF16)
    entries = jnp.dot(
        beam_ref[...].astype(F32).astype(BF16), chosen, preferred_element_type=F32
    ).astype(jnp.int32)
    here = lax.broadcasted_iota(jnp.int32, (MINE, DOMS), 1)
    wanted = lax.broadcasted_iota(jnp.int32, (MINE, DOMS), 0) + section * MINE
    select = jnp.where(here == wanted, 1.0, 0.0).astype(BF16)
    weights = lax.dot_general(select, weight_ref[...], NT, preferred_element_type=F32)
    for j in range(MINE):
        row = jnp.broadcast_to(weights[j : j + 1, :], (BEAMS, LANES))
        for part in range(2):
            for t in range(NSTAT // LANES):
                which = entries[:, LANES * t : LANES * (t + 1)] + part * NTAB
                value = jnp.take_along_axis(row, which, axis=1)
                out_ref[j, pl.ds(part * BEAMS, BEAMS), pl.ds(LANES * t, LANES)] = value.astype(BF16)
    trial = lax.broadcasted_iota(jnp.int32, (NDM, LANES), 0)
    lane = lax.broadcasted_iota(jnp.int32, (NDM, LANES), 1)
    k = lane % FRAMES
    kappa = jnp.where(k < FRAMES // 2, k, k - FRAMES).astype(F32)
    measure = (trial + 1).astype(F32) / NDM
    for j in range(MINE):
        channel = jnp.full((NDM, LANES), dom * (SECTIONS * MINE) + section * MINE + j, jnp.int32)
        freq = 1.0 + channel.astype(F32) / CH
        spread = 1.0 / (freq * freq * freq)
        phase = math.pi * measure * spread * (kappa * kappa / FRAMES)
        sine = jnp.sin(phase)
        tables = []
        for table in (jnp.cos(phase), jnp.where(lane < FRAMES, -sine, sine)):
            top = table.astype(BF16)
            tables += [top, (table - top.astype(F32)).astype(BF16)]
        turn_ref[j] = jnp.concatenate(tables, axis=1)


def prep(station_map, beam_table, weight_table):
    return pl.pallas_call(
        prep_kernel,
        name="prep",
        out_shape=(
            jax.ShapeDtypeStruct((MINE, 2 * BEAMS, NSTAT), BF16),
            jax.ShapeDtypeStruct((MINE, NDM, 4 * LANES), BF16),
        ),
        compiler_params=pltpu.CompilerParams(vmem_limit_bytes=32 << 20),
        cost_estimate=pl.CostEstimate(
            flops=4_000_000_000, bytes_accessed=16 << 20, transcendentals=65536
        ),
    )(
        station_map.reshape(1, NSTAT),
        beam_table,
        weight_table.reshape(2 * NTAB, weight_table.shape[2]),
    )


def split_dot(rows, high, low):
    top = rows.astype(BF16)
    rest = (rows - top.astype(F32)).astype(BF16)
    return (
        jnp.dot(top, high, preferred_element_type=F32)
        + jnp.dot(rest, high, preferred_element_type=F32)
        + jnp.dot(top, low, preferred_element_type=F32)
    )


def beam_kernel(signal_ref, weight_ref, turn_ref, trial_ref, frame_ref, out_ref, series, power):
    column = jnp.broadcast_to(trial_ref[...].astype(F32), (BEAMS, BEAMS)).T[:, :NDM]
    trial = lax.broadcasted_iota(jnp.int32, (BEAMS, NDM), 1).astype(F32)
    onehot = jnp.where(column == trial, 1.0, 0.0).astype(BF16)
    low = lax.broadcasted_iota(jnp.int32, (BEAMS, LANES), 1) < FRAMES
    for j in range(MINE):
        signal = signal_ref[:, pl.ds(j * STATIONS, STATIONS), :].reshape(NSTAT, LANES)
        product = jnp.dot(weight_ref[j], signal, preferred_element_type=F32)
        crossed = pltpu.roll(product[BEAMS:], FRAMES, 1)
        series[pl.ds(j * BEAMS, BEAMS), :] = product[:BEAMS] + jnp.where(low, -crossed, crossed)
    half = MINE // 2
    bins = split_dot(series[...], frame_ref[0], frame_ref[1])
    turns = [jnp.dot(onehot, turn_ref[j], preferred_element_type=F32) for j in range(MINE)]
    turn = jnp.concatenate(turns, axis=0)
    direct = turn[:, :LANES] + turn[:, LANES : 2 * LANES]
    across = turn[:, 2 * LANES : 3 * LANES] + turn[:, 3 * LANES :]
    rotated = bins * direct + pltpu.roll(bins, FRAMES, 1) * across
    result = split_dot(rotated, frame_ref[2], frame_ref[3])
    square = result * result
    found = square + pltpu.roll(square, FRAMES, 1)
    for q in range(half):
        power[pl.ds(q, BEAMS, stride=half), :] = jnp.where(
            low,
            found[q * BEAMS : (q + 1) * BEAMS],
            found[(q + half) * BEAMS : (q + half + 1) * BEAMS],
        )
    out_ref[...] = power[...].astype(BF16)


def form_beams(signal, weights, turns, dm_trial, frames):
    return pl.pallas_call(
        beam_kernel,
        name="beams",
        out_shape=jax.ShapeDtypeStruct((BEAMS * MINE // 2, LANES), BF16),
        scratch_shapes=[
            pltpu.VMEM((MINE * BEAMS, LANES), F32),
            pltpu.VMEM((BEAMS * MINE // 2, LANES), F32),
        ],
        compiler_params=pltpu.CompilerParams(vmem_limit_bytes=24 << 20),
        cost_estimate=pl.CostEstimate(
            flops=400_000_000, bytes_accessed=4 << 20, transcendentals=0
        ),
    )(signal, weights, turns, dm_trial.reshape(1, BEAMS), frames)


def order_kernel(power_ref, out_ref):
    half = MINE // 2
    count = SECTIONS * DOMS * half
    channel = lax.broadcasted_iota(jnp.int32, (count, CH), 1)
    row = lax.broadcasted_iota(jnp.int32, (count, CH), 0)
    owner = channel // (SECTIONS * MINE)
    section = channel // MINE % SECTIONS
    wanted = section * (DOMS * half) + owner * half + channel % half
    place = jnp.where(row == wanted, 1.0, 0.0).astype(BF16)
    turned = power_ref[...].astype(F32).T.astype(BF16)
    placed = jnp.dot(turned, place, preferred_element_type=F32)
    high = lax.broadcasted_iota(jnp.int32, (FRAMES, CH), 1) // half % 2 == 1
    out_ref[0] = jnp.where(high, placed[FRAMES:], placed[:FRAMES])


def order(power):
    return pl.pallas_call(
        order_kernel,
        name="order",
        out_shape=jax.ShapeDtypeStruct((1, FRAMES, CH), F32),
        compiler_params=pltpu.CompilerParams(vmem_limit_bytes=32 << 20),
    )(power)


def body(voltages, station_map, beam_table, weight_table, dm_trial):
    volts = voltages.reshape(STATIONS * FRAMES, NFFT)
    spectra = channelise(jnp.asarray(dft_table()), volts)
    signal = lax.all_to_all(spectra, "dom", split_axis=0, concat_axis=0, tiled=True)
    weights, turns = prep(station_map, beam_table, weight_table)
    power = form_beams(signal, weights, turns, dm_trial, jnp.asarray(frame_tables()))
    power = power.reshape(BEAMS, MINE // 2, LANES)
    power = lax.all_to_all(power, ("section", "dom"), split_axis=0, concat_axis=0, tiled=True)
    return order(power.reshape(BEAMS * MINE // 2, LANES))


def solution(mesh):
    in_specs = (P("dom", None, None), P(), P(), P(None, None, "dom"), P())
    out_specs = P(("section", "dom"), None, None)
    return jax.shard_map(body, mesh=mesh, in_specs=in_specs, out_specs=out_specs, check_vma=False)
```

time: 65.9 us -> 52.6 us (0.80)
  local copies, waits for them, and re-layouts: 8.86 us -> 2.43 us
  Pallas kernels: 17.2 us -> 10.9 us
    unnamed x19 -> x13, local copies, waits for them, and re-layouts: 8.86 us -> 2.43 us
    pallas_call x1, Pallas kernels: 7.13 us -> 1.95 us  [form_beams(): pl.pallas_call(beam_kernel, name='beams', out_shape=jax.ShapeDtypeStruct(...]
    pallas_call x1, Pallas kernels: 6.94 us -> 5.68 us  [channelise(): pl.pallas_call(channelise_kernel, name='channelise', out_shape=jax.ShapeD...]
  transfers between devices with their start and end apart: 1 -> 1, of which waited for: 1 -> 1; matrix products, arithmetic and copies ran while one was open for 0% -> 1% of each run, Pallas kernels for 3% -> 4%
where the time goes in v2:
time: 52.6 us; the launch traced here: 52.3 us
  blocking collectives  16.9 us (32%)
  waiting for transfers between devices  12.2 us (23%)
  Pallas kernels  10.9 us (21%)
  starting transfers between devices  9.82 us (19%)
  local copies, waits for them, and re-layouts  2.43 us (5%)
    all_to_all x1, blocking collectives, body(): lax.all_to_all(power, ('section', 'dom'), split_axis=0, concat_axis=0, ti...  16.9 us
    all_to_all x1, waiting for transfers between devices, body(): lax.all_to_all(spectra, 'dom', split_axis=0, concat_axis=0, tiled=True)  12.2 us
    all_to_all x1, starting transfers between devices, body(): lax.all_to_all(spectra, 'dom', split_axis=0, concat_axis=0, tiled=True)  9.82 us
    pallas_call x1, Pallas kernels, channelise(): pl.pallas_call(channelise_kernel, name='channelise', out_shape=jax.ShapeD...  5.68 us
    unnamed x13, local copies, waits for them, and re-layouts  2.43 us
    pallas_call x1, Pallas kernels, prep(): pl.pallas_call(prep_kernel, name='prep', out_shape=(jax.ShapeDtypeStruct(...  2.1 us
    pallas_call x1, Pallas kernels, form_beams(): pl.pallas_call(beam_kernel, name='beams', out_shape=jax.ShapeDtypeStruct(...  1.95 us
    pallas_call x1, Pallas kernels, order(): pl.pallas_call(order_kernel, name='order', out_shape=jax.ShapeDtypeStruct...  1.13 us
  transfers between devices with their start and end apart: 1, of which 1 were waited for; matrix products, arithmetic and copies ran while one was open for 1% of the time, Pallas kernels for 4%

profile of v2, /device:TPU:1, one launch (start us, length us, event | category | flops | bytes accessed | tf_op | source)
XLA Modules:
  0.0 52.3 jit_solution(16048055527697217743)
XLA Ops:
  0.0 0.0 copy-start.5
  0.0 0.0 copy-start.4
  0.0 5.7 %channelise.1 = bf16[32,128,128]{2,1,0:T(8,128)(2,1)} custom-call(bf16[4,512,2048]{2,1,0:T(8,128)(2,1)} %constant.4.clone.table_hbm, bf16[1024,2048]{1,0:T(8,128)(2,1)} %bitcast.11), custom_call_target="tpu_custom_call" | custom-call | flops 2147483648 | bytes 7340032 | tf_op jit(solution)/shard_map/channelise/pallas_call | solution.py:113
  5.7 9.8 %all-to-all-start = ((bf16[32,128,128]{2,1,0:T(8,128)(2,1)}), bf16[32,128,128]{2,1,0:T(8,128)(2,1)S(1)}, u32[]{:S(2)}, u32[]{:S(2)}) async-start(bf16[32,128,128]{2,1,0:T(8,128)(2,1)} %channelise.1), calls=%async_computation | async-start | bytes 2097152 | tf_op jit(solution)/shard_map/all_to_all | solution.py:273
  15.5 0.0 copy-done.5
  15.5 0.7 %copy.8 = bf16[2,64,32]{2,1,0:T(8,128)(2,1)} copy(bf16[2,64,32]{1,2,0:T(8,128)(2,1)S(1)} %copy-done.5) | data formatting | bytes 16384 | tf_op args[3]
  16.2 0.0 copy-done.4
  16.2 0.0 copy-start.1
  16.3 0.8 %copy-done.1 = bf16[2,64,32]{2,1,0:T(8,128)(2,1)S(1)} copy-done((bf16[2,64,32]{2,1,0:T(8,128)(2,1)S(1)}, bf16[2,64,32]{2,1,0:T(8,128)(2,1)}, u32[]{:S(2)}) %copy-start.1) | copy-done | bytes 8216
  17.0 0.0 copy-start.3
  17.0 0.9 %copy-done.3 = s32[128,512]{1,0:T(8,128)S(1)} copy-done((s32[128,512]{1,0:T(8,128)S(1)}, s32[128,512]{1,0:T(8,128)}, u32[]{:S(2)}) %copy-start.3) | copy-done | bytes 262168
  18.0 0.0 copy-start
  18.0 0.0 copy-start.2
  18.0 2.1 %prep.1 = (bf16[8,256,512]{2,1,0:T(8,128)(2,1)S(1)}, bf16[8,32,512]{2,1,0:T(8,128)(2,1)S(1)}) custom-call(s32[1,512]{1,0:T(1,128)S(1)} %bitcast.10, s32[128,512]{1,0:T(8,128)S(1)} %copy-done.3, bf16[128,32]{1,0:T(8,128)(2,1)S(1)} %bitcast.8), custom_call_target="tpu_custom_call" | custom-call | flops 4000000000 | bytes 16777216 | tf_op jit(solution)/shard_map/prep/pallas_call | solution.py:173
  20.1 12.2 %all-to-all-done.signal_ref = bf16[32,128,128]{2,1,0:T(8,128)(2,1)S(1)} async-done(((bf16[32,128,128]{2,1,0:T(8,128)(2,1)}), bf16[32,128,128]{2,1,0:T(8,128)(2,1)S(1)}, u32[]{:S(2)}, u32[]{:S(2)}) %all-to-all-start) | async-done | bytes 1048608 | tf_op jit(solution)/shard_map/all_to_all | solution.py:273
  32.2 0.0 copy-done
  32.2 0.0 copy-done.2
  32.2 1.9 %beams.1 = bf16[512,128]{1,0:T(8,128)(2,1)S(1)} custom-call(bf16[32,128,128]{2,1,0:T(8,128)(2,1)S(1)} %all-to-all-done.signal_ref, bf16[8,256,512]{2,1,0:T(8,128)(2,1)S(1)} %get-tuple-element.7.weight_ref, bf16[8,32,512]{2,1,0:T(8,128)(2,1)S(1)} %get-tuple-element.8.turn_ref, s32[1,128]{1,0:T(1,128)S(1)} %bitcast.9, bf16[4,128,128]{2,1,0:T(8,128)(2,1)S(1)} %copy-done), custom_call_target="tpu_custom_call" | custom-call | flops 400000000 | bytes 4194304 | tf_op jit(solution)/shard_map/beams/pallas_call | solution.py:231
  34.2 16.9 %all_to_all.10 = bf16[128,4,128]{2,1,0:T(4,128)(2,1)S(1)} all-to-all(bf16[128,4,128]{2,1,0:T(4,128)(2,1)S(1)} %bitcast.6), channel_id=1, replica_groups=mesh['section'=4,'dom'=32] {'section','dom'}, dimensions={0} | all-to-all | bytes 262144 | tf_op jit(solution)/shard_map/all_to_all | solution.py:277
  51.1 1.1 %order.1 = f32[1,64,1024]{2,1,0:T(8,128)} custom-call(bf16[512,128]{1,0:T(8,128)(2,1)S(1)} %bitcast.7), custom_call_target="tpu_custom_call" | custom-call | tf_op jit(solution)/shard_map/order/pallas_call | solution.py:262
Async XLA Ops:
  0.0 15.5 %copy-start.5 = (bf16[2,64,32]{1,2,0:T(8,128)(2,1)S(1)}, bf16[2,64,32]{1,2,0:T(8,128)(2,1)}, u32[]{:S(2)}) copy-start(bf16[2,64,32]{1,2,0:T(8,128)(2,1)} %param.10) | copy-start | bytes 24580
  0.0 16.2 %copy-start.4 = (s32[512]{0:T(512)S(1)}, s32[512]{0:T(512)}, u32[]{:S(2)}) copy-start(s32[512]{0:T(512)} %param.8) | copy-start | bytes 6148
  5.7 26.5 %all-to-all-start = ((bf16[32,128,128]{2,1,0:T(8,128)(2,1)}), bf16[32,128,128]{2,1,0:T(8,128)(2,1)S(1)}, u32[]{:S(2)}, u32[]{:S(2)}) async-start(bf16[32,128,128]{2,1,0:T(8,128)(2,1)} %channelise.1), calls=%async_computation | async-start | bytes 2097152 | tf_op jit(solution)/shard_map/all_to_all | solution.py:273
  16.2 0.8 %copy-start.1 = (bf16[2,64,32]{2,1,0:T(8,128)(2,1)S(1)}, bf16[2,64,32]{2,1,0:T(8,128)(2,1)}, u32[]{:S(2)}) copy-start(bf16[2,64,32]{2,1,0:T(8,128)(2,1)} %copy.8) | copy-start | bytes 24580
  17.0 0.9 %copy-start.3 = (s32[128,512]{1,0:T(8,128)S(1)}, s32[128,512]{1,0:T(8,128)}, u32[]{:S(2)}) copy-start(s32[128,512]{1,0:T(8,128)} %beam_ref.1) | copy-start | bytes 786436
  18.0 14.3 %copy-start = (bf16[4,128,128]{2,1,0:T(8,128)(2,1)S(1)}, bf16[4,128,128]{2,1,0:T(8,128)(2,1)}, u32[]{:S(2)}) copy-start(bf16[4,128,128]{2,1,0:T(8,128)(2,1)} %constant.5.clone.frame_ref) | copy-start | bytes 393220
  18.0 14.3 %copy-start.2 = (s32[128]{0:T(128)S(1)}, s32[128]{0:T(128)}, u32[]{:S(2)}) copy-start(s32[128]{0:T(128)} %param.11) | copy-start | bytes 1540

commit v3 on v2

--- a/solution.py
+++ b/solution.py
@@ -41,17 +41,13 @@
     return parts.reshape(SECTIONS, COLS, NFFT).astype(ml_dtypes.bfloat16)
 
 
-def frame_tables():
+def frame_table():
     index = np.arange(FRAMES)
     angle = (index[:, None] * index[None, :] % FRAMES) * (2.0 * math.pi / FRAMES)
     cosine, sine = np.cos(angle), np.sin(angle)
-    forward = np.block([[cosine, -sine], [sine, cosine]])
-    inverse = np.block([[cosine, sine], [-sine, cosine]]) / FRAMES
-    tables = []
-    for table in (forward, inverse):
-        high = table.astype(ml_dtypes.bfloat16)
-        tables += [high, (table - high.astype(np.float64)).astype(ml_dtypes.bfloat16)]
-    return np.stack(tables)
+    table = np.block([[cosine, -sine], [sine, cosine]])
+    high = table.astype(ml_dtypes.bfloat16)
+    return np.stack((high, (table - high.astype(np.float64)).astype(ml_dtypes.bfloat16)))
 
 
 def channelise_kernel(
@@ -133,13 +129,18 @@
     )(table, volts)
 
 
-def prep_kernel(map_ref, beam_ref, weight_ref, out_ref, turn_ref):
+def prep_kernel(map_ref, beam_ref, weight_ref, trial_ref, out_ref, turn_ref, choice_ref):
     section, dom = lax.axis_index("section"), lax.axis_index("dom")
+    place = lax.broadcasted_iota(jnp.int32, (BEAMS, BEAMS), 0)
+    beam = lax.broadcasted_iota(jnp.int32, (BEAMS, BEAMS), 1)
+    swap = jnp.where(beam == place % SECTIONS * DOMS + place // SECTIONS, 1.0, 0.0).astype(BF16)
     station = lax.broadcasted_iota(jnp.int32, (NSTAT, NSTAT), 0)
     chosen = jnp.where(station == map_ref[...], 1.0, 0.0).astype(BF16)
-    entries = jnp.dot(
-        beam_ref[...].astype(F32).astype(BF16), chosen, preferred_element_type=F32
-    ).astype(jnp.int32)
+    swapped = jnp.dot(swap, beam_ref[...].astype(F32).astype(BF16), preferred_element_type=F32)
+    entries = jnp.dot(swapped.astype(BF16), chosen, preferred_element_type=F32).astype(jnp.int32)
+    wanted = lax.broadcasted_iota(jnp.int32, (2 * NDM, BEAMS), 0) % NDM
+    onehot = jnp.where(wanted == trial_ref[...], 1.0, 0.0).astype(BF16)
+    choice_ref[...] = lax.dot_general(swap, onehot, NT, preferred_element_type=F32).astype(BF16)
     here = lax.broadcasted_iota(jnp.int32, (MINE, DOMS), 1)
     wanted = lax.broadcasted_iota(jnp.int32, (MINE, DOMS), 0) + section * MINE
     select = jnp.where(here == wanted, 1.0, 0.0).astype(BF16)
@@ -162,20 +163,20 @@
         spread = 1.0 / (freq * freq * freq)
         phase = math.pi * measure * spread * (kappa * kappa / FRAMES)
         sine = jnp.sin(phase)
-        tables = []
-        for table in (jnp.cos(phase), jnp.where(lane < FRAMES, -sine, sine)):
-            top = table.astype(BF16)
-            tables += [top, (table - top.astype(F32)).astype(BF16)]
-        turn_ref[j] = jnp.concatenate(tables, axis=1)
-
-
-def prep(station_map, beam_table, weight_table):
+        table = jnp.concatenate((jnp.cos(phase), jnp.where(lane < FRAMES, -sine, sine)), axis=1)
+        top = table.astype(BF16)
+        turn_ref[j, :NDM] = top
+        turn_ref[j, NDM:] = (table - top.astype(F32)).astype(BF16)
+
+
+def prep(station_map, beam_table, weight_table, dm_trial):
     return pl.pallas_call(
         prep_kernel,
         name="prep",
         out_shape=(
             jax.ShapeDtypeStruct((MINE, 2 * BEAMS, NSTAT), BF16),
-            jax.ShapeDtypeStruct((MINE, NDM, 4 * LANES), BF16),
+            jax.ShapeDtypeStruct((MINE, 2 * NDM, 2 * LANES), BF16),
+            jax.ShapeDtypeStruct((BEAMS, 2 * NDM), BF16),
         ),
         compiler_params=pltpu.CompilerParams(vmem_limit_bytes=32 << 20),
         cost_estimate=pl.CostEstimate(
@@ -185,23 +186,31 @@
         station_map.reshape(1, NSTAT),
         beam_table,
         weight_table.reshape(2 * NTAB, weight_table.shape[2]),
-    )
-
-
-def split_dot(rows, high, low):
+        dm_trial.reshape(1, BEAMS),
+    )
+
+
+def split_dot(rows, high, low, turned):
     top = rows.astype(BF16)
     rest = (rows - top.astype(F32)).astype(BF16)
-    return (
-        jnp.dot(top, high, preferred_element_type=F32)
-        + jnp.dot(rest, high, preferred_element_type=F32)
-        + jnp.dot(top, low, preferred_element_type=F32)
-    )
-
-
-def beam_kernel(signal_ref, weight_ref, turn_ref, trial_ref, frame_ref, out_ref, series, power):
-    column = jnp.broadcast_to(trial_ref[...].astype(F32), (BEAMS, BEAMS)).T[:, :NDM]
-    trial = lax.broadcasted_iota(jnp.int32, (BEAMS, NDM), 1).astype(F32)
-    onehot = jnp.where(column == trial, 1.0, 0.0).astype(BF16)
+    side = int(turned)
+    tables = jnp.concatenate(
+        (
+            jnp.concatenate((high, low), axis=1 - side),
+            jnp.concatenate((high, jnp.zeros_like(high)), axis=1 - side),
+        ),
+        axis=side,
+    )
+    both = lax.dot_general(
+        jnp.concatenate((top, rest), axis=1),
+        tables,
+        (((1,), (side,)), ((), ())),
+        preferred_element_type=F32,
+    )
+    return both[:, :LANES] + both[:, LANES:]
+
+
+def beam_kernel(signal_ref, weight_ref, turn_ref, choice_ref, frame_ref, out_ref, series, power):
     low = lax.broadcasted_iota(jnp.int32, (BEAMS, LANES), 1) < FRAMES
     for j in range(MINE):
         signal = signal_ref[:, pl.ds(j * STATIONS, STATIONS), :].reshape(NSTAT, LANES)
@@ -209,13 +218,12 @@
         crossed = pltpu.roll(product[BEAMS:], FRAMES, 1)
         series[pl.ds(j * BEAMS, BEAMS), :] = product[:BEAMS] + jnp.where(low, -crossed, crossed)
     half = MINE // 2
-    bins = split_dot(series[...], frame_ref[0], frame_ref[1])
-    turns = [jnp.dot(onehot, turn_ref[j], preferred_element_type=F32) for j in range(MINE)]
+    bins = split_dot(series[...], frame_ref[0], frame_ref[1], False)
+    choice = choice_ref[...]
+    turns = [jnp.dot(choice, turn_ref[j], preferred_element_type=F32) for j in range(MINE)]
     turn = jnp.concatenate(turns, axis=0)
-    direct = turn[:, :LANES] + turn[:, LANES : 2 * LANES]
-    across = turn[:, 2 * LANES : 3 * LANES] + turn[:, 3 * LANES :]
-    rotated = bins * direct + pltpu.roll(bins, FRAMES, 1) * across
-    result = split_dot(rotated, frame_ref[2], frame_ref[3])
+    rotated = bins * turn[:, :LANES] + pltpu.roll(bins, FRAMES, 1) * turn[:, LANES:]
+    result = split_dot(rotated, frame_ref[0], frame_ref[1], True) * (1.0 / FRAMES)
     square = result * result
     found = square + pltpu.roll(square, FRAMES, 1)
     for q in range(half):
@@ -227,7 +235,7 @@
     out_ref[...] = power[...].astype(BF16)
 
 
-def form_beams(signal, weights, turns, dm_trial, frames):
+def form_beams(signal, weights, turns, choice, frames):
     return pl.pallas_call(
         beam_kernel,
         name="beams",
@@ -240,22 +248,23 @@
         cost_estimate=pl.CostEstimate(
             flops=400_000_000, bytes_accessed=4 << 20, transcendentals=0
         ),
-    )(signal, weights, turns, dm_trial.reshape(1, BEAMS), frames)
+    )(signal, weights, turns, choice, frames)
 
 
 def order_kernel(power_ref, out_ref):
     half = MINE // 2
-    count = SECTIONS * DOMS * half
-    channel = lax.broadcasted_iota(jnp.int32, (count, CH), 1)
-    row = lax.broadcasted_iota(jnp.int32, (count, CH), 0)
-    owner = channel // (SECTIONS * MINE)
-    section = channel // MINE % SECTIONS
-    wanted = section * (DOMS * half) + owner * half + channel % half
-    place = jnp.where(row == wanted, 1.0, 0.0).astype(BF16)
-    turned = power_ref[...].astype(F32).T.astype(BF16)
-    placed = jnp.dot(turned, place, preferred_element_type=F32)
-    high = lax.broadcasted_iota(jnp.int32, (FRAMES, CH), 1) // half % 2 == 1
-    out_ref[0] = jnp.where(high, placed[FRAMES:], placed[:FRAMES])
+    row = lax.broadcasted_iota(jnp.int32, (LANES, 2 * LANES), 0)
+    channel = lax.broadcasted_iota(jnp.int32, (1, 2 * LANES), 1)
+    place = jnp.where(row == channel // MINE * half + channel % half, 1.0, 0.0).astype(BF16)
+    high = lax.broadcasted_iota(jnp.int32, (FRAMES, 2 * LANES), 1) // half % 2 == 1
+    for n in range(CH // (2 * LANES)):
+        rows = power_ref[pl.ds(n * LANES, LANES), :]
+        placed = lax.dot_general(
+            rows, place, (((0,), (0,)), ((), ())), preferred_element_type=F32
+        )
+        out_ref[0, :, pl.ds(n * 2 * LANES, 2 * LANES)] = jnp.where(
+            high, placed[FRAMES:], placed[:FRAMES]
+        )
 
 
 def order(power):
@@ -271,10 +280,10 @@
     volts = voltages.reshape(STATIONS * FRAMES, NFFT)
     spectra = channelise(jnp.asarray(dft_table()), volts)
     signal = lax.all_to_all(spectra, "dom", split_axis=0, concat_axis=0, tiled=True)
-    weights, turns = prep(station_map, beam_table, weight_table)
-    power = form_beams(signal, weights, turns, dm_trial, jnp.asarray(frame_tables()))
+    weights, turns, choice = prep(station_map, beam_table, weight_table, dm_trial)
+    power = form_beams(signal, weights, turns, choice, jnp.asarray(frame_table()))
     power = power.reshape(BEAMS, MINE // 2, LANES)
-    power = lax.all_to_all(power, ("section", "dom"), split_axis=0, concat_axis=0, tiled=True)
+    power = lax.all_to_all(power, ("dom", "section"), split_axis=0, concat_axis=0, tiled=True)
     return order(power.reshape(BEAMS * MINE // 2, LANES))
 
 

time: 52.6 us -> 51.9 us (0.987)
  local copies, waits for them, and re-layouts: 2.43 us -> 1.06 us
  waiting for transfers between devices: 12.2 us -> 13.4 us
  Pallas kernels: 10.9 us -> 10.3 us
    unnamed x13 -> x11, local copies, waits for them, and re-layouts: 2.43 us -> 1.06 us
    all_to_all x1, waiting for transfers between devices: 12.2 us -> 13.4 us  [body(): lax.all_to_all(spectra, 'dom', split_axis=0, concat_axis=0, tiled=True)]
  transfers between devices with their start and end apart: 1 -> 1, of which waited for: 1 -> 1; matrix products, arithmetic and copies ran while one was open for 1% -> 0% of each run, Pallas kernels for 4% -> 4%
where the time goes in v3:
time: 51.9 us; the launch traced here: 51.7 us
  blocking collectives  17 us (33%)
  waiting for transfers between devices  13.4 us (26%)
  Pallas kernels  10.3 us (20%)
  starting transfers between devices  9.83 us (19%)
  local copies, waits for them, and re-layouts  1.06 us (2%)
    all_to_all x1, blocking collectives, body(): lax.all_to_all(power, ('dom', 'section'), split_axis=0, concat_axis=0, ti...  17 us
    all_to_all x1, waiting for transfers between devices, body(): lax.all_to_all(spectra, 'dom', split_axis=0, concat_axis=0, tiled=True)  13.4 us
    all_to_all x1, starting transfers between devices, body(): lax.all_to_all(spectra, 'dom', split_axis=0, concat_axis=0, tiled=True)  9.83 us
    pallas_call x1, Pallas kernels, channelise(): pl.pallas_call(channelise_kernel, name='channelise', out_shape=jax.ShapeD...  5.69 us
    pallas_call x1, Pallas kernels, prep(): pl.pallas_call(prep_kernel, name='prep', out_shape=(jax.ShapeDtypeStruct(...  2.22 us
    pallas_call x1, Pallas kernels, form_beams(): pl.pallas_call(beam_kernel, name='beams', out_shape=jax.ShapeDtypeStruct(...  1.44 us
    unnamed x11, local copies, waits for them, and re-layouts  1.06 us
  transfers between devices with their start and end apart: 1, of which 1 were waited for; matrix products, arithmetic and copies ran while one was open for 0% of the time, Pallas kernels for 4%

profile of v3, /device:TPU:1, one launch (start us, length us, event | category | flops | bytes accessed | tf_op | source)
XLA Modules:
  0.0 51.7 jit_solution(8094438047062970828)
XLA Ops:
  0.0 0.0 copy-start.4
  0.0 0.0 copy-start.2
  0.0 0.0 copy-start.3
  0.0 5.7 %channelise.1 = bf16[32,128,128]{2,1,0:T(8,128)(2,1)} custom-call(bf16[4,512,2048]{2,1,0:T(8,128)(2,1)} %constant.4.clone.table_hbm, bf16[1024,2048]{1,0:T(8,128)(2,1)} %bitcast.11), custom_call_target="tpu_custom_call" | custom-call | flops 2147483648 | bytes 7340032 | tf_op jit(solution)/shard_map/channelise/pallas_call | solution.py:109
  5.7 9.8 %all-to-all-start = ((bf16[32,128,128]{2,1,0:T(8,128)(2,1)}), bf16[32,128,128]{2,1,0:T(8,128)(2,1)S(1)}, u32[]{:S(2)}, u32[]{:S(2)}) async-start(bf16[32,128,128]{2,1,0:T(8,128)(2,1)} %channelise.1), calls=%async_computation | async-start | bytes 2097152 | tf_op jit(solution)/shard_map/all_to_all | solution.py:282
  15.5 0.0 copy-done.4
  15.6 0.1 copy.8
  15.7 0.0 copy-done.2
  15.7 0.0 copy-done.3
  15.7 0.0 copy-start.1
  15.7 0.9 %copy-done.1 = s32[128,512]{1,0:T(8,128)S(1)} copy-done((s32[128,512]{1,0:T(8,128)S(1)}, s32[128,512]{1,0:T(8,128)}, u32[]{:S(2)}) %copy-start.1) | copy-done | bytes 262168
  16.6 0.0 copy-start
  16.6 2.2 %prep.1 = (bf16[8,256,512]{2,1,0:T(8,128)(2,1)S(1)}, bf16[8,64,256]{2,1,0:T(8,128)(2,1)S(1)}, bf16[128,64]{1,0:T(8,128)(2,1)S(1)}) custom-call(s32[1,512]{1,0:T(1,128)S(1)} %bitcast.9, s32[128,512]{1,0:T(8,128)S(1)} %copy-done.1, bf16[128,32]{1,0:T(8,128)(2,1)S(1)} %bitcast.8, s32[1,128]{1,0:T(1,128)S(1)} %bitcast.10), custom_call_target="tpu_custom_call" | custom-call | flops 4000000000 | bytes 16777216 | tf_op jit(solution)/shard_map/prep/pallas_call | solution.py:173
  18.8 13.4 %all-to-all-done.signal_ref = bf16[32,128,128]{2,1,0:T(8,128)(2,1)S(1)} async-done(((bf16[32,128,128]{2,1,0:T(8,128)(2,1)}), bf16[32,128,128]{2,1,0:T(8,128)(2,1)S(1)}, u32[]{:S(2)}, u32[]{:S(2)}) %all-to-all-start) | async-done | bytes 1048608 | tf_op jit(solution)/shard_map/all_to_all | solution.py:282
  32.3 0.0 copy-done
  32.3 1.4 %beams.1 = bf16[512,128]{1,0:T(8,128)(2,1)S(1)} custom-call(bf16[32,128,128]{2,1,0:T(8,128)(2,1)S(1)} %all-to-all-done.signal_ref, bf16[8,256,512]{2,1,0:T(8,128)(2,1)S(1)} %get-tuple-element.8.weight_ref, bf16[8,64,256]{2,1,0:T(8,128)(2,1)S(1)} %get-tuple-element.9.turn_ref, bf16[128,64]{1,0:T(8,128)(2,1)S(1)} %get-tuple-element.10.choice_ref, ...), custom_call_target="tpu_custom_call" | custom-call | flops 400000000 | bytes 4194304 | tf_op jit(solution)/shard_map/beams/pallas_call | solution.py:239
  33.7 17.0 %all_to_all.10 = bf16[128,4,128]{2,1,0:T(4,128)(2,1)S(1)} all-to-all(bf16[128,4,128]{2,1,0:T(4,128)(2,1)S(1)} %bitcast.6), channel_id=1, replica_groups=mesh['section'=4,'dom'=32] {'dom','section'}, dimensions={0} | all-to-all | bytes 262144 | tf_op jit(solution)/shard_map/all_to_all | solution.py:286
  50.7 1.0 %order.1 = f32[1,64,1024]{2,1,0:T(8,128)} custom-call(bf16[512,128]{1,0:T(8,128)(2,1)S(1)} %bitcast.7), custom_call_target="tpu_custom_call" | custom-call | tf_op jit(solution)/shard_map/order/pallas_call | solution.py:271
Async XLA Ops:
  0.0 15.5 %copy-start.4 = (bf16[2,64,32]{1,2,0:T(8,128)(2,1)S(1)}, bf16[2,64,32]{1,2,0:T(8,128)(2,1)}, u32[]{:S(2)}) copy-start(bf16[2,64,32]{1,2,0:T(8,128)(2,1)} %param.10) | copy-start | bytes 24580
  0.0 15.7 %copy-start.2 = (s32[512]{0:T(512)S(1)}, s32[512]{0:T(512)}, u32[]{:S(2)}) copy-start(s32[512]{0:T(512)} %param.8) | copy-start | bytes 6148
  0.0 15.7 %copy-start.3 = (s32[128]{0:T(128)S(1)}, s32[128]{0:T(128)}, u32[]{:S(2)}) copy-start(s32[128]{0:T(128)} %param.11) | copy-start | bytes 1540
  5.7 26.6 %all-to-all-start = ((bf16[32,128,128]{2,1,0:T(8,128)(2,1)}), bf16[32,128,128]{2,1,0:T(8,128)(2,1)S(1)}, u32[]{:S(2)}, u32[]{:S(2)}) async-start(bf16[32,128,128]{2,1,0:T(8,128)(2,1)} %channelise.1), calls=%async_computation | async-start | bytes 2097152 | tf_op jit(solution)/shard_map/all_to_all | solution.py:282
  15.7 1.0 %copy-start.1 = (s32[128,512]{1,0:T(8,128)S(1)}, s32[128,512]{1,0:T(8,128)}, u32[]{:S(2)}) copy-start(s32[128,512]{1,0:T(8,128)} %beam_ref.1) | copy-start | bytes 786436
  16.6 15.6 %copy-start = (bf16[2,128,128]{2,1,0:T(8,128)(2,1)S(1)}, bf16[2,128,128]{2,1,0:T(8,128)(2,1)}, u32[]{:S(2)}) copy-start(bf16[2,128,128]{2,1,0:T(8,128)(2,1)} %constant.5.clone.frame_ref) | copy-start | bytes 196612

commit v4 on v3

--- a/solution.py
+++ b/solution.py
@@ -22,9 +22,13 @@
 MINE = CH // (SECTIONS * DOMS)
 LANES = 128
 COLS = 2 * CH // SECTIONS
+SHARE = SECTIONS * MINE // 2
 STEPS = 4
 PIECE = NFFT // STEPS
 NT = (((1,), (1,)), ((), ()))
+GRID = (4, 4, 2)
+PARTNERS = [int(d) for d in np.arange(DOMS).reshape(GRID).transpose(2, 1, 0).ravel()]
+EVERYONE = [s * DOMS + d for d in PARTNERS for s in range(SECTIONS)]
 F32 = jnp.float32
 BF16 = jnp.bfloat16
 
@@ -37,7 +41,7 @@
         2.0 * math.pi / NFFT
     )
     parts = np.stack((np.cos(angle) * scale, -np.sin(angle) * scale))
-    parts = parts.reshape(2, DOMS, SECTIONS, MINE, NFFT).transpose(2, 1, 0, 3, 4)
+    parts = parts.reshape(2, DOMS, SECTIONS, MINE, NFFT)[:, PARTNERS].transpose(2, 1, 0, 3, 4)
     return parts.reshape(SECTIONS, COLS, NFFT).astype(ml_dtypes.bfloat16)
 
 
@@ -133,7 +137,9 @@
     section, dom = lax.axis_index("section"), lax.axis_index("dom")
     place = lax.broadcasted_iota(jnp.int32, (BEAMS, BEAMS), 0)
     beam = lax.broadcasted_iota(jnp.int32, (BEAMS, BEAMS), 1)
-    swap = jnp.where(beam == place % SECTIONS * DOMS + place // SECTIONS, 1.0, 0.0).astype(BF16)
+    z, y, x = place // 4 % 4, place // 16 % 4, place // 64
+    owner = place % SECTIONS * DOMS + (z * 4 + y) * 2 + x
+    swap = jnp.where(beam == owner, 1.0, 0.0).astype(BF16)
     station = lax.broadcasted_iota(jnp.int32, (NSTAT, NSTAT), 0)
     chosen = jnp.where(station == map_ref[...], 1.0, 0.0).astype(BF16)
     swapped = jnp.dot(swap, beam_ref[...].astype(F32).astype(BF16), preferred_element_type=F32)
@@ -183,7 +189,7 @@
             flops=4_000_000_000, bytes_accessed=16 << 20, transcendentals=65536
         ),
     )(
-        station_map.reshape(1, NSTAT),
+        station_map.reshape(*GRID, STATIONS).transpose(2, 1, 0, 3).reshape(1, NSTAT),
         beam_table,
         weight_table.reshape(2 * NTAB, weight_table.shape[2]),
         dm_trial.reshape(1, BEAMS),
@@ -258,7 +264,10 @@
     place = jnp.where(row == channel // MINE * half + channel % half, 1.0, 0.0).astype(BF16)
     high = lax.broadcasted_iota(jnp.int32, (FRAMES, 2 * LANES), 1) // half % 2 == 1
     for n in range(CH // (2 * LANES)):
-        rows = power_ref[pl.ds(n * LANES, LANES), :]
+        owners = range(n * LANES // SHARE, (n + 1) * LANES // SHARE)
+        rows = jnp.concatenate(
+            [power_ref[pl.ds(PARTNERS.index(d) * SHARE, SHARE), :] for d in owners], axis=0
+        )
         placed = lax.dot_general(
             rows, place, (((0,), (0,)), ((), ())), preferred_element_type=F32
         )
@@ -279,11 +288,20 @@
 def body(voltages, station_map, beam_table, weight_table, dm_trial):
     volts = voltages.reshape(STATIONS * FRAMES, NFFT)
     spectra = channelise(jnp.asarray(dft_table()), volts)
-    signal = lax.all_to_all(spectra, "dom", split_axis=0, concat_axis=0, tiled=True)
+    signal = lax.all_to_all(
+        spectra, "dom", split_axis=0, concat_axis=0, tiled=True, axis_index_groups=[PARTNERS]
+    )
     weights, turns, choice = prep(station_map, beam_table, weight_table, dm_trial)
     power = form_beams(signal, weights, turns, choice, jnp.asarray(frame_table()))
     power = power.reshape(BEAMS, MINE // 2, LANES)
-    power = lax.all_to_all(power, ("dom", "section"), split_axis=0, concat_axis=0, tiled=True)
+    power = lax.all_to_all(
+        power,
+        ("section", "dom"),
+        split_axis=0,
+        concat_axis=0,
+        tiled=True,
+        axis_index_groups=[EVERYONE],
+    )
     return order(power.reshape(BEAMS * MINE // 2, LANES))
 
 

time: 51.9 us -> 51.3 us (0.988)
  waiting for transfers between devices: 13.4 us -> 11.4 us
  blocking collectives: 17 us -> 18.2 us
    all_to_all x1, waiting for transfers between devices: 13.4 us -> 11.4 us  [body(): lax.all_to_all(spectra, 'dom', split_axis=0, concat_axis=0, tiled=True, a...]
    all_to_all x1, blocking collectives: 17 us -> 18.2 us  [body(): lax.all_to_all(power, ('section', 'dom'), split_axis=0, concat_axis=0, ti...]
  transfers between devices with their start and end apart: 1 -> 1, of which waited for: 1 -> 1; matrix products, arithmetic and copies ran while one was open for 0% -> 1% of each run, Pallas kernels for 4% -> 4%
where the time goes in v4:
time: 51.3 us; the launch traced here: 51.1 us
  blocking collectives  18.2 us (35%)
  waiting for transfers between devices  11.4 us (22%)
  Pallas kernels  10.3 us (20%)
  starting transfers between devices  9.83 us (19%)
  local copies, waits for them, and re-layouts  1.24 us (2%)
    all_to_all x1, blocking collectives, body(): lax.all_to_all(power, ('section', 'dom'), split_axis=0, concat_axis=0, ti...  18.2 us
    all_to_all x1, waiting for transfers between devices, body(): lax.all_to_all(spectra, 'dom', split_axis=0, concat_axis=0, tiled=True, a...  11.4 us
    all_to_all x1, starting transfers between devices, body(): lax.all_to_all(spectra, 'dom', split_axis=0, concat_axis=0, tiled=True, a...  9.83 us
    pallas_call x1, Pallas kernels, channelise(): pl.pallas_call(channelise_kernel, name='channelise', out_shape=jax.ShapeD...  5.69 us
    pallas_call x1, Pallas kernels, prep(): pl.pallas_call(prep_kernel, name='prep', out_shape=(jax.ShapeDtypeStruct(...  2.22 us
    pallas_call x1, Pallas kernels, form_beams(): pl.pallas_call(beam_kernel, name='beams', out_shape=jax.ShapeDtypeStruct(...  1.46 us
    unnamed x11, local copies, waits for them, and re-layouts  1.06 us
  transfers between devices with their start and end apart: 1, of which 1 were waited for; matrix products, arithmetic and copies ran while one was open for 1% of the time, Pallas kernels for 4%

profile of v4, /device:TPU:1, one launch (start us, length us, event | category | flops | bytes accessed | tf_op | source)
XLA Modules:
  0.0 51.1 jit_solution(6932125836890571947)
XLA Ops:
  0.0 0.0 copy-start.4
  0.0 0.0 copy-start.3
  0.0 0.0 copy-start.2
  0.0 5.7 %channelise.1 = bf16[32,128,128]{2,1,0:T(8,128)(2,1)} custom-call(bf16[4,512,2048]{2,1,0:T(8,128)(2,1)} %constant.4.clone.table_hbm, bf16[1024,2048]{1,0:T(8,128)(2,1)} %bitcast.10), custom_call_target="tpu_custom_call" | custom-call | flops 2147483648 | bytes 7340032 | tf_op jit(solution)/shard_map/channelise/pallas_call | solution.py:113
  5.7 9.8 %all-to-all-start = ((bf16[32,128,128]{2,1,0:T(8,128)(2,1)}), bf16[32,128,128]{2,1,0:T(8,128)(2,1)S(1)}, u32[]{:S(2)}, u32[]{:S(2)}) async-start(bf16[32,128,128]{2,1,0:T(8,128)(2,1)} %channelise.1), calls=%async_computation | async-start | bytes 2097152 | tf_op jit(solution)/shard_map/all_to_all | solution.py:291
  15.5 0.0 copy-done.4
  15.6 0.1 reshape.22
  15.7 0.1 reshape.23.map_ref
  15.7 0.0 copy-done.3
  15.7 0.1 copy.10
  15.9 0.0 copy-done.2
  15.9 0.0 copy-start.1
  15.9 0.9 %copy-done.1 = s32[128,512]{1,0:T(8,128)S(1)} copy-done((s32[128,512]{1,0:T(8,128)S(1)}, s32[128,512]{1,0:T(8,128)}, u32[]{:S(2)}) %copy-start.1) | copy-done | bytes 262168
  16.8 0.0 copy-start
  16.8 2.2 %prep.1 = (bf16[8,256,512]{2,1,0:T(8,128)(2,1)S(1)}, bf16[8,64,256]{2,1,0:T(8,128)(2,1)S(1)}, bf16[128,64]{1,0:T(8,128)(2,1)S(1)}) custom-call(s32[1,512]{1,0:T(1,128)S(1)} %reshape.23.map_ref, s32[128,512]{1,0:T(8,128)S(1)} %copy-done.1, bf16[128,32]{1,0:T(8,128)(2,1)S(1)} %bitcast.8, s32[1,128]{1,0:T(1,128)S(1)} %bitcast.9), custom_call_target="tpu_custom_call" | custom-call | flops 4000000000 | bytes 16777216 | tf_op jit(solution)/shard_map/prep/pallas_call | solution.py:179
  19.0 11.4 %all-to-all-done.signal_ref = bf16[32,128,128]{2,1,0:T(8,128)(2,1)S(1)} async-done(((bf16[32,128,128]{2,1,0:T(8,128)(2,1)}), bf16[32,128,128]{2,1,0:T(8,128)(2,1)S(1)}, u32[]{:S(2)}, u32[]{:S(2)}) %all-to-all-start) | async-done | bytes 1048608 | tf_op jit(solution)/shard_map/all_to_all | solution.py:291
  30.4 0.0 copy-done
  30.4 1.5 %beams.1 = bf16[512,128]{1,0:T(8,128)(2,1)S(1)} custom-call(bf16[32,128,128]{2,1,0:T(8,128)(2,1)S(1)} %all-to-all-done.signal_ref, bf16[8,256,512]{2,1,0:T(8,128)(2,1)S(1)} %get-tuple-element.8.weight_ref, bf16[8,64,256]{2,1,0:T(8,128)(2,1)S(1)} %get-tuple-element.9.turn_ref, bf16[128,64]{1,0:T(8,128)(2,1)S(1)} %get-tuple-element.10.choice_ref, ...), custom_call_target="tpu_custom_call" | custom-call | flops 400000000 | bytes 4194304 | tf_op jit(solution)/shard_map/beams/pallas_call | solution.py:245
  31.9 18.2 %all_to_all.10 = bf16[128,4,128]{2,1,0:T(4,128)(2,1)S(1)} all-to-all(bf16[128,4,128]{2,1,0:T(4,128)(2,1)S(1)} %bitcast.6), channel_id=1, replica_groups={{0,32,64,96,8,40,72,104,16,48,80,112,24,56,88,120,2,34,66,98,10,42,74,1..., dimensions={0} | all-to-all | bytes 262144 | tf_op jit(solution)/shard_map/all_to_all | solution.py:297
  50.1 1.0 %order.1 = f32[1,64,1024]{2,1,0:T(8,128)} custom-call(bf16[512,128]{1,0:T(8,128)(2,1)S(1)} %bitcast.7), custom_call_target="tpu_custom_call" | custom-call | tf_op jit(solution)/shard_map/order/pallas_call | solution.py:280
  (1 shorter events, 0.0 us)
Async XLA Ops:
  0.0 15.5 %copy-start.4 = (s32[512]{0:T(512)S(1)}, s32[512]{0:T(512)}, u32[]{:S(2)}) copy-start(s32[512]{0:T(512)} %param.8) | copy-start | bytes 6148
  0.0 15.7 %copy-start.3 = (bf16[2,64,32]{1,2,0:T(8,128)(2,1)S(1)}, bf16[2,64,32]{1,2,0:T(8,128)(2,1)}, u32[]{:S(2)}) copy-start(bf16[2,64,32]{1,2,0:T(8,128)(2,1)} %param.10) | copy-start | bytes 24580
  0.0 15.8 %copy-start.2 = (s32[128]{0:T(128)S(1)}, s32[128]{0:T(128)}, u32[]{:S(2)}) copy-start(s32[128]{0:T(128)} %param.11) | copy-start | bytes 1540
  5.7 24.7 %all-to-all-start = ((bf16[32,128,128]{2,1,0:T(8,128)(2,1)}), bf16[32,128,128]{2,1,0:T(8,128)(2,1)S(1)}, u32[]{:S(2)}, u32[]{:S(2)}) async-start(bf16[32,128,128]{2,1,0:T(8,128)(2,1)} %channelise.1), calls=%async_computation | async-start | bytes 2097152 | tf_op jit(solution)/shard_map/all_to_all | solution.py:291
  15.9 1.0 %copy-start.1 = (s32[128,512]{1,0:T(8,128)S(1)}, s32[128,512]{1,0:T(8,128)}, u32[]{:S(2)}) copy-start(s32[128,512]{1,0:T(8,128)} %beam_ref.1) | copy-start | bytes 786436
  16.8 13.6 %copy-start = (bf16[2,128,128]{2,1,0:T(8,128)(2,1)S(1)}, bf16[2,128,128]{2,1,0:T(8,128)(2,1)}, u32[]{:S(2)}) copy-start(bf16[2,128,128]{2,1,0:T(8,128)(2,1)} %constant.5.clone.frame_ref) | copy-start | bytes 196612

commit v5 on v4

--- a/solution.py
+++ b/solution.py
@@ -24,6 +24,7 @@
 COLS = 2 * CH // SECTIONS
 SHARE = SECTIONS * MINE // 2
 STEPS = 4
+STORES = 4
 PIECE = NFFT // STEPS
 NT = (((1,), (1,)), ((), ()))
 GRID = (4, 4, 2)
@@ -82,28 +83,26 @@
     for load in loads[-1]:
         load.wait()
     low = lax.broadcasted_iota(jnp.int32, (8, LANES), 1) < FRAMES
-    for part in range(2):
-        rows = pl.ds(part * COLS // 2, COLS // 2)
-        spectrum = total[rows, :] + lax.dot_general(
-            table[rows, pieces[-1]], volts[:, pieces[-1]], NT, preferred_element_type=F32
-        )
-        for d in range(DOMS // 2):
-            for t in range(STATIONS // 2):
-                real = spectrum[16 * d : 16 * d + 8, LANES * t : LANES * (t + 1)]
-                imag = spectrum[16 * d + 8 : 16 * d + 16, LANES * t : LANES * (t + 1)]
-                base = (part * DOMS // 2 + d) * MINE * STATIONS + 2 * t
-                turned[pl.ds(base, 8, stride=STATIONS), :] = jnp.where(
-                    low, real, pltpu.roll(imag, FRAMES, 1)
-                )
-                turned[pl.ds(base + 1, 8, stride=STATIONS), :] = jnp.where(
-                    low, pltpu.roll(real, FRAMES, 1), imag
-                )
+    spectrum = total[...] + lax.dot_general(
+        table[:, pieces[-1]], volts[:, pieces[-1]], NT, preferred_element_type=F32
+    )
+    for d in range(DOMS):
+        for t in range(STATIONS // 2):
+            real = spectrum[16 * d : 16 * d + 8, LANES * t : LANES * (t + 1)]
+            imag = spectrum[16 * d + 8 : 16 * d + 16, LANES * t : LANES * (t + 1)]
+            base = d * MINE * STATIONS + 2 * t
+            turned[pl.ds(base, 8, stride=STATIONS), :] = jnp.where(
+                low, real, pltpu.roll(imag, FRAMES, 1)
+            )
+            turned[pl.ds(base + 1, 8, stride=STATIONS), :] = jnp.where(
+                low, pltpu.roll(real, FRAMES, 1), imag
+            )
     stores = []
-    for part in range(2):
-        half = pl.ds(part * DOMS // 2, DOMS // 2)
-        for d in range(part * DOMS // 2, (part + 1) * DOMS // 2):
+    for part in range(STORES):
+        group = pl.ds(part * DOMS // STORES, DOMS // STORES)
+        for d in range(part * DOMS // STORES, (part + 1) * DOMS // STORES):
             out[d] = turned[pl.ds(d * LANES, LANES), :].astype(BF16)
-        stores.append(pltpu.make_async_copy(out.at[half], out_hbm.at[half], out_sem.at[part]))
+        stores.append(pltpu.make_async_copy(out.at[group], out_hbm.at[group], out_sem.at[part]))
         stores[-1].start()
     for store in stores:
         store.wait()
@@ -124,7 +123,7 @@
             pltpu.VMEM((DOMS, MINE * STATIONS, LANES), BF16),
             pltpu.SemaphoreType.DMA((STEPS,)),
             pltpu.SemaphoreType.DMA((STEPS,)),
-            pltpu.SemaphoreType.DMA((2,)),
+            pltpu.SemaphoreType.DMA((STORES,)),
         ],
         compiler_params=pltpu.CompilerParams(vmem_limit_bytes=61 << 20),
         cost_estimate=pl.CostEstimate(
@@ -257,12 +256,13 @@
     )(signal, weights, turns, choice, frames)
 
 
-def order_kernel(power_ref, out_ref):
+def order_kernel(power_ref, out_hbm, out, sems):
     half = MINE // 2
     row = lax.broadcasted_iota(jnp.int32, (LANES, 2 * LANES), 0)
     channel = lax.broadcasted_iota(jnp.int32, (1, 2 * LANES), 1)
     place = jnp.where(row == channel // MINE * half + channel % half, 1.0, 0.0).astype(BF16)
     high = lax.broadcasted_iota(jnp.int32, (FRAMES, 2 * LANES), 1) // half % 2 == 1
+    copies = []
     for n in range(CH // (2 * LANES)):
         owners = range(n * LANES // SHARE, (n + 1) * LANES // SHARE)
         rows = jnp.concatenate(
@@ -271,9 +271,14 @@
         placed = lax.dot_general(
             rows, place, (((0,), (0,)), ((), ())), preferred_element_type=F32
         )
-        out_ref[0, :, pl.ds(n * 2 * LANES, 2 * LANES)] = jnp.where(
-            high, placed[FRAMES:], placed[:FRAMES]
-        )
+        block = pl.ds(n * 2 * LANES, 2 * LANES)
+        out[0, :, block] = jnp.where(high, placed[FRAMES:], placed[:FRAMES])
+        copies.append(
+            pltpu.make_async_copy(out.at[:, :, block], out_hbm.at[:, :, block], sems.at[n])
+        )
+        copies[-1].start()
+    for copy in copies:
+        copy.wait()
 
 
 def order(power):
@@ -281,6 +286,11 @@
         order_kernel,
         name="order",
         out_shape=jax.ShapeDtypeStruct((1, FRAMES, CH), F32),
+        out_specs=pl.BlockSpec(memory_space=pl.ANY),
+        scratch_shapes=[
+            pltpu.VMEM((1, FRAMES, CH), F32),
+            pltpu.SemaphoreType.DMA((CH // (2 * LANES),)),
+        ],
         compiler_params=pltpu.CompilerParams(vmem_limit_bytes=32 << 20),
     )(power)
 

time: 51.3 us -> 51.3 us (level)
  no operation moved by 1% of the time
where the time goes in v5:
time: 51.3 us; the launch traced here: 51 us
  blocking collectives  18.2 us (35%)
  waiting for transfers between devices  11.4 us (22%)
  Pallas kernels  10.2 us (20%)
  starting transfers between devices  9.83 us (19%)
  local copies, waits for them, and re-layouts  1.24 us (2%)
    all_to_all x1, blocking collectives, body(): lax.all_to_all(power, ('section', 'dom'), split_axis=0, concat_axis=0, ti...  18.2 us
    all_to_all x1, waiting for transfers between devices, body(): lax.all_to_all(spectra, 'dom', split_axis=0, concat_axis=0, tiled=True, a...  11.4 us
    all_to_all x1, starting transfers between devices, body(): lax.all_to_all(spectra, 'dom', split_axis=0, concat_axis=0, tiled=True, a...  9.83 us
    pallas_call x1, Pallas kernels, channelise(): pl.pallas_call(channelise_kernel, name='channelise', out_shape=jax.ShapeD...  5.62 us
    pallas_call x1, Pallas kernels, prep(): pl.pallas_call(prep_kernel, name='prep', out_shape=(jax.ShapeDtypeStruct(...  2.22 us
    pallas_call x1, Pallas kernels, form_beams(): pl.pallas_call(beam_kernel, name='beams', out_shape=jax.ShapeDtypeStruct(...  1.46 us
    unnamed x11, local copies, waits for them, and re-layouts  1.06 us
  transfers between devices with their start and end apart: 1, of which 1 were waited for; matrix products, arithmetic and copies ran while one was open for 1% of the time, Pallas kernels for 4%

profile of v5, /device:TPU:1, one launch (start us, length us, event | category | flops | bytes accessed | tf_op | source)
XLA Modules:
  0.0 51.0 jit_solution(9374521012057119113)
XLA Ops:
  0.0 0.0 copy-start.4
  0.0 0.0 copy-start.3
  0.0 0.0 copy-start.2
  0.0 5.6 %channelise.1 = bf16[32,128,128]{2,1,0:T(8,128)(2,1)} custom-call(bf16[4,512,2048]{2,1,0:T(8,128)(2,1)} %constant.4.clone.table_hbm, bf16[1024,2048]{1,0:T(8,128)(2,1)} %bitcast.10), custom_call_target="tpu_custom_call" | custom-call | flops 2147483648 | bytes 7340032 | tf_op jit(solution)/shard_map/channelise/pallas_call | solution.py:112
  5.6 9.8 %all-to-all-start = ((bf16[32,128,128]{2,1,0:T(8,128)(2,1)}), bf16[32,128,128]{2,1,0:T(8,128)(2,1)S(1)}, u32[]{:S(2)}, u32[]{:S(2)}) async-start(bf16[32,128,128]{2,1,0:T(8,128)(2,1)} %channelise.1), calls=%async_computation | async-start | bytes 2097152 | tf_op jit(solution)/shard_map/all_to_all | solution.py:301
  15.5 0.0 copy-done.4
  15.5 0.1 reshape.22
  15.6 0.1 reshape.23.map_ref
  15.7 0.0 copy-done.3
  15.7 0.1 copy.10
  15.8 0.0 copy-done.2
  15.8 0.0 copy-start.1
  15.8 0.9 %copy-done.1 = s32[128,512]{1,0:T(8,128)S(1)} copy-done((s32[128,512]{1,0:T(8,128)S(1)}, s32[128,512]{1,0:T(8,128)}, u32[]{:S(2)}) %copy-start.1) | copy-done | bytes 262168
  16.7 0.0 copy-start
  16.7 2.2 %prep.1 = (bf16[8,256,512]{2,1,0:T(8,128)(2,1)S(1)}, bf16[8,64,256]{2,1,0:T(8,128)(2,1)S(1)}, bf16[128,64]{1,0:T(8,128)(2,1)S(1)}) custom-call(s32[1,512]{1,0:T(1,128)S(1)} %reshape.23.map_ref, s32[128,512]{1,0:T(8,128)S(1)} %copy-done.1, bf16[128,32]{1,0:T(8,128)(2,1)S(1)} %bitcast.8, s32[1,128]{1,0:T(1,128)S(1)} %bitcast.9), custom_call_target="tpu_custom_call" | custom-call | flops 4000000000 | bytes 16777216 | tf_op jit(solution)/shard_map/prep/pallas_call | solution.py:178
  19.0 11.4 %all-to-all-done.signal_ref = bf16[32,128,128]{2,1,0:T(8,128)(2,1)S(1)} async-done(((bf16[32,128,128]{2,1,0:T(8,128)(2,1)}), bf16[32,128,128]{2,1,0:T(8,128)(2,1)S(1)}, u32[]{:S(2)}, u32[]{:S(2)}) %all-to-all-start) | async-done | bytes 1048608 | tf_op jit(solution)/shard_map/all_to_all | solution.py:301
  30.4 0.0 copy-done
  30.4 1.5 %beams.1 = bf16[512,128]{1,0:T(8,128)(2,1)S(1)} custom-call(bf16[32,128,128]{2,1,0:T(8,128)(2,1)S(1)} %all-to-all-done.signal_ref, bf16[8,256,512]{2,1,0:T(8,128)(2,1)S(1)} %get-tuple-element.8.weight_ref, bf16[8,64,256]{2,1,0:T(8,128)(2,1)S(1)} %get-tuple-element.9.turn_ref, bf16[128,64]{1,0:T(8,128)(2,1)S(1)} %get-tuple-element.10.choice_ref, ...), custom_call_target="tpu_custom_call" | custom-call | flops 400000000 | bytes 4194304 | tf_op jit(solution)/shard_map/beams/pallas_call | solution.py:244
  31.8 18.2 %all_to_all.10 = bf16[128,4,128]{2,1,0:T(4,128)(2,1)S(1)} all-to-all(bf16[128,4,128]{2,1,0:T(4,128)(2,1)S(1)} %bitcast.6), channel_id=1, replica_groups={{0,32,64,96,8,40,72,104,16,48,80,112,24,56,88,120,2,34,66,98,10,42,74,1..., dimensions={0} | all-to-all | bytes 262144 | tf_op jit(solution)/shard_map/all_to_all | solution.py:307
  50.1 0.9 %order.1 = f32[1,64,1024]{2,1,0:T(8,128)} custom-call(bf16[512,128]{1,0:T(8,128)(2,1)S(1)} %bitcast.7), custom_call_target="tpu_custom_call" | custom-call | tf_op jit(solution)/shard_map/order/pallas_call | solution.py:285
  (1 shorter events, 0.0 us)
Async XLA Ops:
  0.0 15.5 %copy-start.4 = (s32[512]{0:T(512)S(1)}, s32[512]{0:T(512)}, u32[]{:S(2)}) copy-start(s32[512]{0:T(512)} %param.8) | copy-start | bytes 6148
  0.0 15.7 %copy-start.3 = (bf16[2,64,32]{1,2,0:T(8,128)(2,1)S(1)}, bf16[2,64,32]{1,2,0:T(8,128)(2,1)}, u32[]{:S(2)}) copy-start(bf16[2,64,32]{1,2,0:T(8,128)(2,1)} %param.10) | copy-start | bytes 24580
  0.0 15.8 %copy-start.2 = (s32[128]{0:T(128)S(1)}, s32[128]{0:T(128)}, u32[]{:S(2)}) copy-start(s32[128]{0:T(128)} %param.11) | copy-start | bytes 1540
  5.6 24.7 %all-to-all-start = ((bf16[32,128,128]{2,1,0:T(8,128)(2,1)}), bf16[32,128,128]{2,1,0:T(8,128)(2,1)S(1)}, u32[]{:S(2)}, u32[]{:S(2)}) async-start(bf16[32,128,128]{2,1,0:T(8,128)(2,1)} %channelise.1), calls=%async_computation | async-start | bytes 2097152 | tf_op jit(solution)/shard_map/all_to_all | solution.py:301
  15.8 1.0 %copy-start.1 = (s32[128,512]{1,0:T(8,128)S(1)}, s32[128,512]{1,0:T(8,128)}, u32[]{:S(2)}) copy-start(s32[128,512]{1,0:T(8,128)} %beam_ref.1) | copy-start | bytes 786436
  16.7 13.6 %copy-start = (bf16[2,128,128]{2,1,0:T(8,128)(2,1)S(1)}, bf16[2,128,128]{2,1,0:T(8,128)(2,1)}, u32[]{:S(2)}) copy-start(bf16[2,128,128]{2,1,0:T(8,128)(2,1)} %constant.5.clone.frame_ref) | copy-start | bytes 196612

commit v6 on v5

--- a/solution.py
+++ b/solution.py
@@ -27,8 +27,11 @@
 STORES = 4
 PIECE = NFFT // STEPS
 NT = (((1,), (1,)), ((), ()))
-GRID = (4, 4, 2)
-PARTNERS = [int(d) for d in np.arange(DOMS).reshape(GRID).transpose(2, 1, 0).ravel()]
+TN = (((0,), (0,)), ((), ()))
+PARTNERS = [
+    19, 31, 24, 9, 12, 2, 28, 8, 15, 17, 18, 26, 29, 6, 22, 20,
+    14, 10, 3, 25, 11, 4, 21, 27, 30, 7, 5, 1, 23, 16, 0, 13,
+]
 EVERYONE = [s * DOMS + d for d in PARTNERS for s in range(SECTIONS)]
 F32 = jnp.float32
 BF16 = jnp.bfloat16
@@ -132,20 +135,19 @@
     )(table, volts)
 
 
-def prep_kernel(map_ref, beam_ref, weight_ref, trial_ref, out_ref, turn_ref, choice_ref):
+def prep_kernel(map_ref, owner_ref, beam_ref, weight_ref, trial_ref, out_ref, turn_ref, choice_ref):
     section, dom = lax.axis_index("section"), lax.axis_index("dom")
-    place = lax.broadcasted_iota(jnp.int32, (BEAMS, BEAMS), 0)
-    beam = lax.broadcasted_iota(jnp.int32, (BEAMS, BEAMS), 1)
-    z, y, x = place // 4 % 4, place // 16 % 4, place // 64
-    owner = place % SECTIONS * DOMS + (z * 4 + y) * 2 + x
-    swap = jnp.where(beam == owner, 1.0, 0.0).astype(BF16)
+    beam = lax.broadcasted_iota(jnp.int32, (BEAMS, BEAMS), 0)
+    swap = jnp.where(beam == owner_ref[...], 1.0, 0.0).astype(BF16)
     station = lax.broadcasted_iota(jnp.int32, (NSTAT, NSTAT), 0)
     chosen = jnp.where(station == map_ref[...], 1.0, 0.0).astype(BF16)
-    swapped = jnp.dot(swap, beam_ref[...].astype(F32).astype(BF16), preferred_element_type=F32)
+    table = beam_ref[...].astype(F32).astype(BF16)
+    swapped = lax.dot_general(swap, table, TN, preferred_element_type=F32)
     entries = jnp.dot(swapped.astype(BF16), chosen, preferred_element_type=F32).astype(jnp.int32)
     wanted = lax.broadcasted_iota(jnp.int32, (2 * NDM, BEAMS), 0) % NDM
     onehot = jnp.where(wanted == trial_ref[...], 1.0, 0.0).astype(BF16)
-    choice_ref[...] = lax.dot_general(swap, onehot, NT, preferred_element_type=F32).astype(BF16)
+    choice = lax.dot_general(swap, onehot, (((0,), (1,)), ((), ())), preferred_element_type=F32)
+    choice_ref[...] = choice.astype(BF16)
     here = lax.broadcasted_iota(jnp.int32, (MINE, DOMS), 1)
     wanted = lax.broadcasted_iota(jnp.int32, (MINE, DOMS), 0) + section * MINE
     select = jnp.where(here == wanted, 1.0, 0.0).astype(BF16)
@@ -175,6 +177,7 @@
 
 
 def prep(station_map, beam_table, weight_table, dm_trial):
+    rows = station_map.reshape(DOMS, STATIONS)
     return pl.pallas_call(
         prep_kernel,
         name="prep",
@@ -188,7 +191,8 @@
             flops=4_000_000_000, bytes_accessed=16 << 20, transcendentals=65536
         ),
     )(
-        station_map.reshape(*GRID, STATIONS).transpose(2, 1, 0, 3).reshape(1, NSTAT),
+        jnp.concatenate([rows[d] for d in PARTNERS]).reshape(1, NSTAT),
+        jnp.asarray(np.array(EVERYONE, np.int32).reshape(1, BEAMS)),
         beam_table,
         weight_table.reshape(2 * NTAB, weight_table.shape[2]),
         dm_trial.reshape(1, BEAMS),
@@ -269,7 +273,7 @@
             [power_ref[pl.ds(PARTNERS.index(d) * SHARE, SHARE), :] for d in owners], axis=0
         )
         placed = lax.dot_general(
-            rows, place, (((0,), (0,)), ((), ())), preferred_element_type=F32
+            rows, place, TN, preferred_element_type=F32
         )
         block = pl.ds(n * 2 * LANES, 2 * LANES)
         out[0, :, block] = jnp.where(high, placed[FRAMES:], placed[:FRAMES])

time: 51.3 us -> 50.9 us (level)
  starting transfers between devices: 9.83 us -> 11 us
  blocking collectives: 18.2 us -> 17.3 us
  waiting for transfers between devices: 11.4 us -> 10.6 us
    all_to_all x1, starting transfers between devices: 9.83 us -> 11 us  [body(): lax.all_to_all(spectra, 'dom', split_axis=0, concat_axis=0, tiled=True, a...]
    all_to_all x1, blocking collectives: 18.2 us -> 17.3 us  [body(): lax.all_to_all(power, ('section', 'dom'), split_axis=0, concat_axis=0, ti...]
    all_to_all x1, waiting for transfers between devices: 11.4 us -> 10.6 us  [body(): lax.all_to_all(spectra, 'dom', split_axis=0, concat_axis=0, tiled=True, a...]
    unnamed x11 -> x13, local copies, waits for them, and re-layouts: 1.06 us -> 1.07 us
  transfers between devices with their start and end apart: 1 -> 1, of which waited for: 1 -> 1; matrix products, arithmetic and copies ran while one was open for 1% -> 1% of each run, Pallas kernels for 4% -> 5%
where the time goes in v6:
time: 50.9 us; the launch traced here: 50.6 us
  blocking collectives  17.3 us (34%)
  starting transfers between devices  11 us (22%)
  waiting for transfers between devices  10.6 us (21%)
  Pallas kernels  10.3 us (20%)
  local copies, waits for them, and re-layouts  1.4 us (3%)
    all_to_all x1, blocking collectives, body(): lax.all_to_all(power, ('section', 'dom'), split_axis=0, concat_axis=0, ti...  17.3 us
    all_to_all x1, starting transfers between devices, body(): lax.all_to_all(spectra, 'dom', split_axis=0, concat_axis=0, tiled=True, a...  11 us
    all_to_all x1, waiting for transfers between devices, body(): lax.all_to_all(spectra, 'dom', split_axis=0, concat_axis=0, tiled=True, a...  10.6 us
    pallas_call x1, Pallas kernels, channelise(): pl.pallas_call(channelise_kernel, name='channelise', out_shape=jax.ShapeD...  5.63 us
    pallas_call x1, Pallas kernels, prep(): pl.pallas_call(prep_kernel, name='prep', out_shape=(jax.ShapeDtypeStruct(...  2.29 us
    pallas_call x1, Pallas kernels, form_beams(): pl.pallas_call(beam_kernel, name='beams', out_shape=jax.ShapeDtypeStruct(...  1.45 us
    unnamed x13, local copies, waits for them, and re-layouts  1.07 us
  transfers between devices with their start and end apart: 1, of which 1 were waited for; matrix products, arithmetic and copies ran while one was open for 1% of the time, Pallas kernels for 5%

profile of v6, /device:TPU:1, one launch (start us, length us, event | category | flops | bytes accessed | tf_op | source)
XLA Modules:
  0.0 50.6 jit_solution(1167912176573723855)
XLA Ops:
  0.0 0.0 copy-start.4
  0.0 0.0 copy-start.5
  0.0 0.0 copy-start.2
  0.0 0.0 copy-start.3
  0.0 5.6 %channelise.1 = bf16[32,128,128]{2,1,0:T(8,128)(2,1)} custom-call(bf16[4,512,2048]{2,1,0:T(8,128)(2,1)} %constant.6.clone.table_hbm, bf16[1024,2048]{1,0:T(8,128)(2,1)} %bitcast.11), custom_call_target="tpu_custom_call" | custom-call | flops 2147483648 | bytes 7340032 | tf_op jit(solution)/shard_map/channelise/pallas_call | solution.py:115
  5.7 11.0 %all-to-all-start = ((bf16[32,128,128]{2,1,0:T(8,128)(2,1)}), bf16[32,128,128]{2,1,0:T(8,128)(2,1)S(1)}, u32[]{:S(2)}, u32[]{:S(2)}) async-start(bf16[32,128,128]{2,1,0:T(8,128)(2,1)} %channelise.1), calls=%async_computation | async-start | bytes 2097152 | tf_op jit(solution)/shard_map/all_to_all | solution.py:305
  16.6 0.0 copy-done.4
  16.6 0.1 slice.136
  16.7 0.0 copy-done.5
  16.7 0.1 copy.9
  16.8 0.1 fusion.1
  16.9 0.1 fusion
  17.0 0.1 concatenate.4
  17.1 0.0 copy-done.2
  17.1 0.0 copy-done.3
  17.1 0.0 copy-start.1
  17.1 0.9 %copy-done.1 = s32[128,512]{1,0:T(8,128)S(1)} copy-done((s32[128,512]{1,0:T(8,128)S(1)}, s32[128,512]{1,0:T(8,128)}, u32[]{:S(2)}) %copy-start.1) | copy-done | bytes 262168
  18.1 0.0 copy-start
  18.1 2.3 %prep.1 = (bf16[8,256,512]{2,1,0:T(8,128)(2,1)S(1)}, bf16[8,64,256]{2,1,0:T(8,128)(2,1)S(1)}, bf16[128,64]{1,0:T(8,128)(2,1)S(1)}) custom-call(s32[1,512]{1,0:T(1,128)S(1)} %bitcast.9, s32[1,128]{1,0:T(1,128)S(1)} %copy-done.3, s32[128,512]{1,0:T(8,128)S(1)} %copy-done.1, bf16[128,32]{1,0:T(8,128)(2,1)S(1)} %bitcast.8, s32[1,128]{1,0:T(1,128)S(1)} %bitcast.10), custom_call_target="tpu_custom_call" | custom-call | flops 4000000000 | bytes 16777216 | tf_op jit(solution)/shard_map/prep/pallas_call | solution.py:181
  20.4 10.6 %all-to-all-done.signal_ref = bf16[32,128,128]{2,1,0:T(8,128)(2,1)S(1)} async-done(((bf16[32,128,128]{2,1,0:T(8,128)(2,1)}), bf16[32,128,128]{2,1,0:T(8,128)(2,1)S(1)}, u32[]{:S(2)}, u32[]{:S(2)}) %all-to-all-start) | async-done | bytes 1048608 | tf_op jit(solution)/shard_map/all_to_all | solution.py:305
  30.9 0.0 copy-done
  30.9 1.4 %beams.1 = bf16[512,128]{1,0:T(8,128)(2,1)S(1)} custom-call(bf16[32,128,128]{2,1,0:T(8,128)(2,1)S(1)} %all-to-all-done.signal_ref, bf16[8,256,512]{2,1,0:T(8,128)(2,1)S(1)} %get-tuple-element.8.weight_ref, bf16[8,64,256]{2,1,0:T(8,128)(2,1)S(1)} %get-tuple-element.9.turn_ref, bf16[128,64]{1,0:T(8,128)(2,1)S(1)} %get-tuple-element.10.choice_ref, ...), custom_call_target="tpu_custom_call" | custom-call | flops 400000000 | bytes 4194304 | tf_op jit(solution)/shard_map/beams/pallas_call | solution.py:248
  32.4 17.3 %all_to_all.10 = bf16[128,4,128]{2,1,0:T(4,128)(2,1)S(1)} all-to-all(bf16[128,4,128]{2,1,0:T(4,128)(2,1)S(1)} %bitcast.6), channel_id=1, replica_groups={{19,51,83,115,31,63,95,127,24,56,88,120,9,41,73,105,12,44,76,108,2,34,6..., dimensions={0} | all-to-all | bytes 262144 | tf_op jit(solution)/shard_map/all_to_all | solution.py:311
  49.7 0.9 %order.1 = f32[1,64,1024]{2,1,0:T(8,128)} custom-call(bf16[512,128]{1,0:T(8,128)(2,1)S(1)} %bitcast.7), custom_call_target="tpu_custom_call" | custom-call | tf_op jit(solution)/shard_map/order/pallas_call | solution.py:289
Async XLA Ops:
  0.0 16.6 %copy-start.4 = (s32[512]{0:T(512)S(1)}, s32[512]{0:T(512)}, u32[]{:S(2)}) copy-start(s32[512]{0:T(512)} %param.9) | copy-start | bytes 6148
  0.0 16.7 %copy-start.5 = (bf16[2,64,32]{1,2,0:T(8,128)(2,1)S(1)}, bf16[2,64,32]{1,2,0:T(8,128)(2,1)}, u32[]{:S(2)}) copy-start(bf16[2,64,32]{1,2,0:T(8,128)(2,1)} %param.11) | copy-start | bytes 24580
  0.0 17.1 %copy-start.2 = (s32[128]{0:T(128)S(1)}, s32[128]{0:T(128)}, u32[]{:S(2)}) copy-start(s32[128]{0:T(128)} %param.12) | copy-start | bytes 1540
  0.0 17.1 %copy-start.3 = (s32[1,128]{1,0:T(1,128)S(1)}, s32[1,128]{1,0:T(1,128)}, u32[]{:S(2)}) copy-start(s32[1,128]{1,0:T(1,128)} %constant.7.clone.owner_ref) | copy-start | bytes 1540
  5.7 25.2 %all-to-all-start = ((bf16[32,128,128]{2,1,0:T(8,128)(2,1)}), bf16[32,128,128]{2,1,0:T(8,128)(2,1)S(1)}, u32[]{:S(2)}, u32[]{:S(2)}) async-start(bf16[32,128,128]{2,1,0:T(8,128)(2,1)} %channelise.1), calls=%async_computation | async-start | bytes 2097152 | tf_op jit(solution)/shard_map/all_to_all | solution.py:305
  17.1 1.0 %copy-start.1 = (s32[128,512]{1,0:T(8,128)S(1)}, s32[128,512]{1,0:T(8,128)}, u32[]{:S(2)}) copy-start(s32[128,512]{1,0:T(8,128)} %beam_ref.1) | copy-start | bytes 786436
  18.1 12.8 %copy-start = (bf16[2,128,128]{2,1,0:T(8,128)(2,1)S(1)}, bf16[2,128,128]{2,1,0:T(8,128)(2,1)}, u32[]{:S(2)}) copy-start(bf16[2,128,128]{2,1,0:T(8,128)(2,1)} %constant.8.clone.frame_ref) | copy-start | bytes 196612

commit v7 on v6

--- a/solution.py
+++ b/solution.py
@@ -24,13 +24,13 @@
 COLS = 2 * CH // SECTIONS
 SHARE = SECTIONS * MINE // 2
 STEPS = 4
-STORES = 4
+STORES = 8
 PIECE = NFFT // STEPS
 NT = (((1,), (1,)), ((), ()))
 TN = (((0,), (0,)), ((), ()))
 PARTNERS = [
-    19, 31, 24, 9, 12, 2, 28, 8, 15, 17, 18, 26, 29, 6, 22, 20,
-    14, 10, 3, 25, 11, 4, 21, 27, 30, 7, 5, 1, 23, 16, 0, 13,
+    27, 2, 11, 21, 0, 3, 14, 9, 6, 13, 1, 12, 23, 4, 29, 25,
+    18, 31, 22, 19, 24, 5, 16, 17, 30, 15, 8, 28, 26, 7, 20, 10,
 ]
 EVERYONE = [s * DOMS + d for d in PARTNERS for s in range(SECTIONS)]
 F32 = jnp.float32

time: 50.9 us -> 50.6 us (level)
  starting transfers between devices: 11 us -> 10.1 us
  blocking collectives: 17.3 us -> 17.9 us
    all_to_all x1, starting transfers between devices: 11 us -> 10.1 us  [body(): lax.all_to_all(spectra, 'dom', split_axis=0, concat_axis=0, tiled=True, a...]
    all_to_all x1, blocking collectives: 17.3 us -> 17.9 us  [body(): lax.all_to_all(power, ('section', 'dom'), split_axis=0, concat_axis=0, ti...]
where the time goes in v7:
time: 50.6 us; the launch traced here: 50.3 us
  blocking collectives  17.9 us (35%)
  waiting for transfers between devices  10.6 us (21%)
  Pallas kernels  10.3 us (20%)
  starting transfers between devices  10.1 us (20%)
  local copies, waits for them, and re-layouts  1.34 us (3%)
    all_to_all x1, blocking collectives, body(): lax.all_to_all(power, ('section', 'dom'), split_axis=0, concat_axis=0, ti...  17.9 us
    all_to_all x1, waiting for transfers between devices, body(): lax.all_to_all(spectra, 'dom', split_axis=0, concat_axis=0, tiled=True, a...  10.6 us
    all_to_all x1, starting transfers between devices, body(): lax.all_to_all(spectra, 'dom', split_axis=0, concat_axis=0, tiled=True, a...  10.1 us
    pallas_call x1, Pallas kernels, channelise(): pl.pallas_call(channelise_kernel, name='channelise', out_shape=jax.ShapeD...  5.61 us
    pallas_call x1, Pallas kernels, prep(): pl.pallas_call(prep_kernel, name='prep', out_shape=(jax.ShapeDtypeStruct(...  2.29 us
    pallas_call x1, Pallas kernels, form_beams(): pl.pallas_call(beam_kernel, name='beams', out_shape=jax.ShapeDtypeStruct(...  1.44 us
    unnamed x13, local copies, waits for them, and re-layouts  1.07 us
  transfers between devices with their start and end apart: 1, of which 1 were waited for; matrix products, arithmetic and copies ran while one was open for 1% of the time, Pallas kernels for 5%

profile of v7, /device:TPU:1, one launch (start us, length us, event | category | flops | bytes accessed | tf_op | source)
XLA Modules:
  0.0 50.3 jit_solution(12522441425056617443)
XLA Ops:
  0.0 0.0 copy-start.4
  0.0 0.0 copy-start.5
  0.0 0.0 copy-start.2
  0.0 0.0 copy-start.3
  0.0 5.6 %channelise.1 = bf16[32,128,128]{2,1,0:T(8,128)(2,1)} custom-call(bf16[4,512,2048]{2,1,0:T(8,128)(2,1)} %constant.6.clone.table_hbm, bf16[1024,2048]{1,0:T(8,128)(2,1)} %bitcast.11), custom_call_target="tpu_custom_call" | custom-call | flops 2147483648 | bytes 7340032 | tf_op jit(solution)/shard_map/channelise/pallas_call | solution.py:115
  5.6 10.1 %all-to-all-start = ((bf16[32,128,128]{2,1,0:T(8,128)(2,1)}), bf16[32,128,128]{2,1,0:T(8,128)(2,1)S(1)}, u32[]{:S(2)}, u32[]{:S(2)}) async-start(bf16[32,128,128]{2,1,0:T(8,128)(2,1)} %channelise.1), calls=%async_computation | async-start | bytes 2097152 | tf_op jit(solution)/shard_map/all_to_all | solution.py:305
  15.8 0.0 copy-done.4
  15.8 0.0 copy-done.5
  15.8 0.1 copy.9
  15.9 0.1 fusion.1
  16.0 0.1 fusion
  16.1 0.1 concatenate.4
  16.2 0.0 copy-done.2
  16.2 0.0 copy-done.3
  16.2 0.0 copy-start.1
  16.2 0.9 %copy-done.1 = s32[128,512]{1,0:T(8,128)S(1)} copy-done((s32[128,512]{1,0:T(8,128)S(1)}, s32[128,512]{1,0:T(8,128)}, u32[]{:S(2)}) %copy-start.1) | copy-done | bytes 262168
  17.2 0.0 copy-start
  17.2 2.3 %prep.1 = (bf16[8,256,512]{2,1,0:T(8,128)(2,1)S(1)}, bf16[8,64,256]{2,1,0:T(8,128)(2,1)S(1)}, bf16[128,64]{1,0:T(8,128)(2,1)S(1)}) custom-call(s32[1,512]{1,0:T(1,128)S(1)} %bitcast.9, s32[1,128]{1,0:T(1,128)S(1)} %copy-done.3, s32[128,512]{1,0:T(8,128)S(1)} %copy-done.1, bf16[128,32]{1,0:T(8,128)(2,1)S(1)} %bitcast.8, s32[1,128]{1,0:T(1,128)S(1)} %bitcast.10), custom_call_target="tpu_custom_call" | custom-call | flops 4000000000 | bytes 16777216 | tf_op jit(solution)/shard_map/prep/pallas_call | solution.py:181
  19.5 10.6 %all-to-all-done.signal_ref = bf16[32,128,128]{2,1,0:T(8,128)(2,1)S(1)} async-done(((bf16[32,128,128]{2,1,0:T(8,128)(2,1)}), bf16[32,128,128]{2,1,0:T(8,128)(2,1)S(1)}, u32[]{:S(2)}, u32[]{:S(2)}) %all-to-all-start) | async-done | bytes 1048608 | tf_op jit(solution)/shard_map/all_to_all | solution.py:305
  30.1 0.0 copy-done
  30.1 1.4 %beams.1 = bf16[512,128]{1,0:T(8,128)(2,1)S(1)} custom-call(bf16[32,128,128]{2,1,0:T(8,128)(2,1)S(1)} %all-to-all-done.signal_ref, bf16[8,256,512]{2,1,0:T(8,128)(2,1)S(1)} %get-tuple-element.8.weight_ref, bf16[8,64,256]{2,1,0:T(8,128)(2,1)S(1)} %get-tuple-element.9.turn_ref, bf16[128,64]{1,0:T(8,128)(2,1)S(1)} %get-tuple-element.10.choice_ref, ...), custom_call_target="tpu_custom_call" | custom-call | flops 400000000 | bytes 4194304 | tf_op jit(solution)/shard_map/beams/pallas_call | solution.py:248
  31.5 17.9 %all_to_all.10 = bf16[128,4,128]{2,1,0:T(4,128)(2,1)S(1)} all-to-all(bf16[128,4,128]{2,1,0:T(4,128)(2,1)S(1)} %bitcast.6), channel_id=1, replica_groups={{27,59,91,123,2,34,66,98,11,43,75,107,21,53,85,117,0,32,64,96,3,35,67,9..., dimensions={0} | all-to-all | bytes 262144 | tf_op jit(solution)/shard_map/all_to_all | solution.py:311
  49.4 0.9 %order.1 = f32[1,64,1024]{2,1,0:T(8,128)} custom-call(bf16[512,128]{1,0:T(8,128)(2,1)S(1)} %bitcast.7), custom_call_target="tpu_custom_call" | custom-call | tf_op jit(solution)/shard_map/order/pallas_call | solution.py:289
  (1 shorter events, 0.0 us)
Async XLA Ops:
  0.0 15.8 %copy-start.4 = (s32[512]{0:T(512)S(1)}, s32[512]{0:T(512)}, u32[]{:S(2)}) copy-start(s32[512]{0:T(512)} %param.9) | copy-start | bytes 6148
  0.0 15.8 %copy-start.5 = (bf16[2,64,32]{1,2,0:T(8,128)(2,1)S(1)}, bf16[2,64,32]{1,2,0:T(8,128)(2,1)}, u32[]{:S(2)}) copy-start(bf16[2,64,32]{1,2,0:T(8,128)(2,1)} %param.11) | copy-start | bytes 24580
  0.0 16.2 %copy-start.2 = (s32[128]{0:T(128)S(1)}, s32[128]{0:T(128)}, u32[]{:S(2)}) copy-start(s32[128]{0:T(128)} %param.12) | copy-start | bytes 1540
  0.0 16.2 %copy-start.3 = (s32[1,128]{1,0:T(1,128)S(1)}, s32[1,128]{1,0:T(1,128)}, u32[]{:S(2)}) copy-start(s32[1,128]{1,0:T(1,128)} %constant.7.clone.owner_ref) | copy-start | bytes 1540
  5.6 24.4 %all-to-all-start = ((bf16[32,128,128]{2,1,0:T(8,128)(2,1)}), bf16[32,128,128]{2,1,0:T(8,128)(2,1)S(1)}, u32[]{:S(2)}, u32[]{:S(2)}) async-start(bf16[32,128,128]{2,1,0:T(8,128)(2,1)} %channelise.1), calls=%async_computation | async-start | bytes 2097152 | tf_op jit(solution)/shard_map/all_to_all | solution.py:305
  16.2 1.0 %copy-start.1 = (s32[128,512]{1,0:T(8,128)S(1)}, s32[128,512]{1,0:T(8,128)}, u32[]{:S(2)}) copy-start(s32[128,512]{1,0:T(8,128)} %beam_ref.1) | copy-start | bytes 786436
  17.2 12.9 %copy-start = (bf16[2,128,128]{2,1,0:T(8,128)(2,1)S(1)}, bf16[2,128,128]{2,1,0:T(8,128)(2,1)}, u32[]{:S(2)}) copy-start(bf16[2,128,128]{2,1,0:T(8,128)(2,1)} %constant.8.clone.frame_ref) | copy-start | bytes 196612
